TPU v7x, 32 devices: a whole 2x2x4 slice. The times are simulated.
32 devices in a mesh: var: 8 (over z, y), samp: 4 (over x, core).
Axes of the slice: x: 2, y: 2, z: 4, core: 2. Of those that a mesh axis runs over, the one named last changes fastest.
Arguments:
- dosage: bfloat16 [16384, 4096], P('samp', 'var'), may hold values from 0 to 2
- pair_offsets: int32 [8, 3], P('var'), may hold values from -1 to 2, as said below
- live_counts: int32 [8], P('var'), may hold values from 256 to 512, as said below
Outputs:
- ld_upper: bfloat16 [8, 3, 512, 512], P('var', None, 'samp')
- ld_mirror: bfloat16 [8, 2, 512, 512], P('var', None, 'samp')
Inputs may be any that keep to these rules, and one draw needn't show every extreme that they name: `pair_offsets`: row i lists distinct offsets in increasing order, first always 0, each with i + offset < 8; unused slots at the end hold -1. The first live_counts[i] variants of block i are real, the rest of the block is padding and is left out.
All inputs are finite; a program needn't handle non-finite values.
Results may differ from a plain program's by a relative error of at most 0.0034.
Values may be sent and summed in bfloat16 or wider, within the bound.
No kernel may reach another device: no remote copies, remote signals or barrier semaphores. Data moves between devices by JAX's collectives and lax.ppermute only.
A program may use at most 320 MiB of HBM per device.

v0:
```python
import jax
import jax.numpy as jnp
from jax import lax
from jax.experimental import pallas as pl
from jax.experimental.pallas import tpu as pltpu
from jax.sharding import PartitionSpec as P

SLOTS = 3
AXES = ("var", "samp")
F32 = jnp.float32
BF16 = jnp.bfloat16
VMEM = pl.BlockSpec(memory_space=pltpu.VMEM)
SMEM = pl.BlockSpec(memory_space=pltpu.SMEM)
BIG = pltpu.CompilerParams(vmem_limit_bytes=56 << 20)
D_BLOCKS = {0: [(0, 0)], 1: [(0, 1), (1, 0), (1, 1)]}


def dot(a, b):
    return jnp.dot(a, b, preferred_element_type=F32)


def standardized(raw, stat_ref):
    return ((raw.astype(F32) - stat_ref[0:1, :]) * stat_ref[1:2, :]).astype(BF16)


def first_kernel(steps, x_ref, chunk_0, chunk_1, out_ref, center, total, square):
    step = pl.program_id(0)
    rows, width = x_ref.shape
    strip = chunk_0.shape[1] // 2
    group = min(64, rows)
    for part, out in enumerate((chunk_0, chunk_1)):
        for half in range(2):
            start = (2 * half + part) * strip
            out[:, half * strip:(half + 1) * strip] = x_ref[:, start:start + strip]

    @pl.when(step == 0)
    def _():
        center[...] = jnp.mean(x_ref[:group, :].astype(F32), axis=0, keepdims=True)
        total[...] = jnp.zeros_like(total)
        square[...] = jnp.zeros_like(square)

    middle = center[...]

    def add(i, sums):
        x = x_ref[pl.ds(pl.multiple_of(i * group, group), group), :].astype(F32) - middle
        x = x.reshape(group // 8, 8, width)
        return sums[0] + jnp.sum(x, axis=0), sums[1] + jnp.sum(x * x, axis=0)

    sums = lax.fori_loop(0, rows // group, add, (total[...], square[...]))
    total[...], square[...] = sums

    @pl.when(step == pl.num_programs(0) - 1)
    def _():
        count = float(rows * steps)
        shift = jnp.sum(total[...], axis=0, keepdims=True) * (1.0 / count)
        around = jnp.sum(square[...], axis=0, keepdims=True) - shift * shift * count
        out_ref[0:1, :] = middle + shift
        out_ref[1:2, :] = jnp.maximum(around, 0.0)


def stat_kernel(pos_ref, live_ref, offsets_ref, own_ref, sib_ref, far_ref, cross_ref, plain_ref, chunked_ref):
    width = own_ref.shape[1]
    strip = width // 4
    samples = pos_ref[4].astype(F32)

    def merged(values):
        return (values[0] + values[1]) + (values[2] + values[3])

    groups = (own_ref, sib_ref, far_ref, cross_ref)
    mean = merged([ref[0:1, :] for ref in groups]) * 0.25
    between = merged([jnp.square(ref[0:1, :] - mean) for ref in groups]) * (samples * 0.25)
    spread = (merged([ref[1:2, :] for ref in groups]) + between) / samples
    live = lax.broadcasted_iota(jnp.int32, (1, width), 1) < live_ref[0]
    plain_ref[0:1, :] = mean
    plain_ref[1:2, :] = jnp.where(live, lax.rsqrt(spread + 1e-05), 0.0)
    for step in (1, 2):
        listed = offsets_ref[0, 0] == step
        for slot in range(1, SLOTS):
            listed = jnp.logical_or(listed, offsets_ref[0, slot] == step)
        plain_ref[1 + step:2 + step, :] = jnp.full((1, width), jnp.where(listed, 1.0, 0.0), F32)
    for part in range(2):
        for half in range(2):
            start, to = (2 * half + part) * strip, (2 * part + half) * strip
            chunked_ref[:, to:to + strip] = plain_ref[:, start:start + strip]


def own_kernel(pos_ref, x_ref, stat_ref, turned_ref, keep_ref, send_ref, acc):
    step = pl.program_id(0)
    z = standardized(x_ref[...], stat_ref)
    zt = z.T
    turned_ref[...] = zt
    part = dot(zt, z)

    @pl.when(step == 0)
    def _():
        acc[...] = part

    @pl.when(step > 0)
    def _():
        acc[...] += part

    @pl.when(step == pl.num_programs(0) - 1)
    def _():
        half = keep_ref.shape[0]
        keep_ref[...] = acc[pl.ds(pl.multiple_of(pos_ref[0] * half, half), half), :]
        send_ref[...] = acc[pl.ds(pl.multiple_of((1 - pos_ref[0]) * half, half), half), :]


def put_blocks(x, source, base, out_keep, out_send, first, parts):
    size = out_keep.shape[-1]
    for out, near in ((out_keep, x), (out_send, 1 - x)):
        index = first
        for r, h in ((near, near), (near, 1 - near), (1 - near, near)):
            for part in range(parts):
                row = pl.multiple_of(r * parts * size + part * size, size)
                col = pl.multiple_of(base + h * size, size)
                out[index] = source[pl.ds(row, size), pl.ds(col, size)].astype(out.dtype)
                index += 1


def pair_kernel(chunk, *refs):
    (pos_ref, turned_ref, y_ref, w_ref, stat_ref, ystat_ref, wstat_ref), refs = refs[:7], refs[7:]
    if chunk == 0:
        keep_c, send_c, keep_bd, send_bd, yt_out, w_out, acc_b, acc_c, acc_d = refs
    else:
        yt_old, w_old, keep_c, send_c, keep_bd, send_bd, acc_b, acc_c, acc_d, acc_e = refs
    step = pl.program_id(0)
    last = pl.num_programs(0) - 1
    x = pos_ref[0]
    active = pos_ref[1] == 1
    size = keep_c.shape[-1]

    @pl.when(step == 0)
    def _():
        for acc in (acc_b, acc_c, acc_d) + (() if chunk == 0 else (acc_e,)):
            acc[...] = jnp.zeros_like(acc)

    zt = turned_ref[...]
    w = standardized(w_ref[...], wstat_ref)
    acc_c[...] += dot(zt, w)
    if chunk == 0:
        w_out[...] = w

    @pl.when(active)
    def _():
        y = standardized(y_ref[...], ystat_ref)
        yt = y.T
        acc_b[...] += dot(zt, y)
        if chunk == 0:
            yt_out[...] = yt
            acc_d[...] += dot(yt, w)
        else:
            acc_e[...] += dot(yt_old[...], w)
            acc_d[:, :2 * size] += dot(yt, w_old[...])
            acc_d[:, 2 * size:] += dot(yt, w)

    @pl.when(step == last)
    def _():
        first = pos_ref[2] == 0
        share = 1.0 / pos_ref[4].astype(F32)
        acc_c[...] *= jnp.where(first, stat_ref[3:4, :], wstat_ref[3:4, :]) * share
        put_blocks(x, acc_c, 0, keep_c, send_c, 0, 2)

        @pl.when(active)
        def _():
            acc_b[...] *= jnp.where(first, stat_ref[2:3, :], ystat_ref[2:3, :]) * share
            put_blocks(x, acc_b, 0, keep_bd, send_bd, 0, 2)
            scale = jnp.where(first, ystat_ref[2:3, :], wstat_ref[2:3, :]) * share
            acc_d[:, :2 * size] *= scale
            if chunk == 0:
                put_blocks(x, acc_d, 0, keep_bd, send_bd, 6, 1)
            else:
                acc_d[:, 2 * size:] *= scale
                acc_e[...] *= scale
                put_blocks(x, acc_e, 0, keep_bd, send_bd, 6, 1)
                put_blocks(x, acc_d, 0, keep_bd, send_bd, 9, 1)
                put_blocks(x, acc_d, 2 * size, keep_bd, send_bd, 12, 1)


def strips_kernel(chunk, pos_ref, keep_c, got_c, keep_bd, got_bd, held_b, held_c, to_y, to_z):
    size = keep_c.shape[-1]
    x = pos_ref[0]

    def at(half, part):
        return pl.ds(pl.multiple_of(half * 2 * size + part * size, size), size)

    def summed(keep, got, index):
        return keep[index] + got[index].astype(F32)

    def side(keep, got, held, out):
        for core in range(2):
            for first, half in ((0, x), (2, 1 - x)):
                held[core, :, pl.ds(pl.multiple_of(half * size, size), size)] = summed(keep, got, first + core)
            for first, half in ((0, x), (4, 1 - x)):
                out[:, at(half, core)] = summed(keep, got, first + core).T.astype(out.dtype)

    side(keep_c, got_c, held_c, to_z)

    @pl.when(pos_ref[1] == 1)
    def _():
        side(keep_bd, got_bd, held_b, to_y)
        for index in range(len(D_BLOCKS[chunk])):
            near, right, below = [summed(keep_bd, got_bd, 6 + 3 * index + which) for which in range(3)]
            start = (4 + 2 * index) * size
            to_y[:, start:start + size] = near.astype(to_y.dtype)
            to_y[:, start + size:start + 2 * size] = right.astype(to_y.dtype)
            to_z[:, start:start + size] = near.T.astype(to_z.dtype)
            to_z[:, start + size:start + 2 * size] = below.T.astype(to_z.dtype)


def combine_kernel(pos_ref, held_b0, held_c0, held_b1, held_c1, y_0, z_0, y_1, z_1, diag_keep, diag_got, mine, sib):
    size = held_b0.shape[1]
    x = pos_ref[0]
    active = pos_ref[1]

    def at(half, part):
        return pl.ds(pl.multiple_of(half * 2 * size + part * size, size), size)

    def fill(core, out):
        def total(index, helds, side):
            for part, held in enumerate(helds):
                for half in range(2):
                    cols = slice((2 * half + part) * size, (2 * half + part + 1) * size)
                    out[index, :, cols] = (held[core, :, half * size:(half + 1) * size] + side[:, cols].astype(F32))

        def far(pieces, sides):
            for part in range(2):
                block = pieces(part)
                chunk = max(block)
                start = (4 + 2 * D_BLOCKS[chunk].index(block)) * size
                out[2, :, at(x, part)] = sides[chunk][:, start:start + size].astype(F32)
                out[2, :, at(1 - x, part)] = sides[chunk][:, start + size:start + 2 * size].astype(F32)

        total(1, (held_c0, held_c1), (z_0, z_1)[core])

        @pl.when(active == 1)
        def _():
            total(0, (held_b0, held_b1), (y_0, y_1)[core])
            far(lambda part: (core, part), (y_0, y_1))

        @pl.when(active == 0)
        def _():
            far(lambda part: (part, core), (z_0, z_1))

        rows = slice(core * size, (core + 1) * size)
        out[3] = diag_keep[rows, :] + diag_got[rows, :]

    for core in range(2):
        @pl.when(pos_ref[2] == core)
        def _():
            fill(core, mine)
            fill(1 - core, sib)


def finish_kernel(pos_ref, offsets_ref, mine, sib, upper, mirror):
    active = pos_ref[1] == 1
    first_core = pos_ref[2] == 0
    even = pos_ref[3] == 0
    pick = jnp.where
    near = pick(active, mine[0], sib[0])
    far = mine[2] + sib[2]
    upper_1 = pick(even, near, far)
    upper_2 = pick(first_core, mine[1], sib[1])
    mirror[0, 0] = pick(even, far, near).astype(BF16)
    mirror[0, 1] = pick(first_core, sib[1], mine[1]).astype(BF16)
    self_tile = (mine[3] + sib[3]) * (1.0 / pos_ref[4].astype(F32))
    for slot in range(SLOTS):
        offset = offsets_ref[0, slot]
        tile = pick(offset == 0, self_tile, pick(offset == 1, upper_1, pick(offset == 2, upper_2, 0.0)))
        upper[0, slot] = tile.astype(BF16)


def body(dosage, pair_offsets, live_counts):
    n_var = lax.axis_size("var")
    n_samp = lax.axis_size("samp")
    depth, width = dosage.shape
    half = width // 2
    strip = width // n_samp
    samples_all = depth * n_samp
    v = lax.axis_index("var")
    s = lax.axis_index("samp")
    x, core, odd = s // 2, s % 2, v % 2
    active = (core == odd).astype(jnp.int32)

    def at(var, samp):
        return var * n_samp + samp

    def active_on(var, samp):
        return var % 2 == samp % 2

    everyone = [(var, samp) for var in range(n_var) for samp in range(n_samp)]
    z_main = [(at(a, b), at(a - 2 if b % 2 == 0 else a + 2, b)) for a, b in everyone
              if 0 <= (a - 2 if b % 2 == 0 else a + 2) < n_var]
    y_main = [(at(a, b), at(a ^ 1, b)) for a, b in everyone if not active_on(a, b)]
    across = [(at(a, b), at(a, b ^ 2)) for a, b in everyone]
    across_active = [(at(a, b), at(a, b ^ 2)) for a, b in everyone if active_on(a, b)]
    sibling = [(at(a, b), at(a, b ^ 1)) for a, b in everyone]

    def send(value, pairs):
        return lax.ppermute(value, AXES, pairs)

    pos = jnp.stack([x, active, core, odd, jnp.int32(samples_all), s]).astype(jnp.int32)
    step_rows = min(1024, depth)
    steps = depth // step_rows
    tall = pl.BlockSpec((step_rows, half), lambda k: (k, 0))
    wide = pl.BlockSpec((step_rows, width), lambda k: (k, 0))
    flat = lambda rows: pl.BlockSpec((rows, step_rows), lambda k: (0, k))
    whole = lambda *shape: pl.BlockSpec(shape, lambda k: (0,) * len(shape))

    chunk_0, chunk_1, local = pl.pallas_call(
        lambda *refs: first_kernel(steps, *refs),
        grid=(steps,),
        in_specs=[wide],
        out_specs=[tall, tall, whole(2, width)],
        out_shape=[jax.ShapeDtypeStruct((depth, half), BF16)] * 2 + [jax.ShapeDtypeStruct((2, width), F32)],
        scratch_shapes=[pltpu.VMEM((1, width), F32)] + [pltpu.VMEM((8, width), F32)] * 2,
        compiler_params=BIG,
        cost_estimate=pl.CostEstimate(flops=5 * depth * width, bytes_accessed=4 * depth * width, transcendentals=0),
        name="chunks_and_local_stats",
    )(dosage)
    w_raw, y_raw = [send(chunk_0, z_main)], [send(chunk_0, y_main)]
    others = [send(local, [(at(a, b), at(a, b ^ flip)) for a, b in everyone]) for flip in (1, 2, 3)]
    stat, stat_chunked = pl.pallas_call(
        stat_kernel,
        in_specs=[SMEM, SMEM, SMEM] + [VMEM] * 4,
        out_specs=[VMEM, VMEM],
        out_shape=[jax.ShapeDtypeStruct((4, width), F32)] * 2,
        name="stats",
    )(pos, live_counts, pair_offsets, local, *others)
    stat, chunk_1 = lax.optimization_barrier((stat, chunk_1))
    w_raw.append(send(chunk_1, z_main))
    y_raw.append(send(chunk_1, y_main))
    z_step = [(a, b, a + 2 if b % 2 == 0 else a - 2) for a, b in everyone]
    z_cross = [(at(a, b), at(t, b ^ 1)) for a, b, t in z_step if 0 <= t < n_var]
    y_cross = [(at(a, b), at(a ^ 1, b ^ 1)) for a, b in everyone if active_on(a, b)]
    w_stat, y_stat = send(stat_chunked, z_cross), send(stat_chunked, y_cross)

    turned, diag_keep, diag_send = pl.pallas_call(
        own_kernel,
        grid=(steps,),
        in_specs=[SMEM, wide, whole(4, width)],
        out_specs=[flat(width)] + [whole(half, width)] * 2,
        out_shape=[jax.ShapeDtypeStruct((width, depth), BF16)] + [jax.ShapeDtypeStruct((half, width), F32)] * 2,
        scratch_shapes=[pltpu.VMEM((width, width), F32)],
        compiler_params=BIG,
        cost_estimate=pl.CostEstimate(flops=2 * depth * width * width, bytes_accessed=4 * depth * width, transcendentals=0),
        name="own_tile",
    )(pos, dosage, stat)
    diag_across = send(diag_send, across)
    keeps, arrived, passed, before = [], [], [], [diag_across]
    sent_as = (F32, BF16)
    for part in range(2):
        n_bd = 6 + 3 * len(D_BLOCKS[part])
        in_specs = [SMEM, flat(width), tall, tall] + [pl.BlockSpec((4, half), lambda k, part=part: (0, part))] * 3
        out_specs = [whole(6, strip, strip)] * 2 + [whole(n_bd, strip, strip)] * 2
        out_shape = [jax.ShapeDtypeStruct((n, strip, strip), kind) for n in (6, n_bd) for kind in (F32, sent_as[part])]
        scratch = [pltpu.VMEM((width, half), F32)] * 2
        if part == 0:
            out_specs += [flat(half), tall]
            out_shape += [jax.ShapeDtypeStruct((half, depth), BF16), jax.ShapeDtypeStruct((depth, half), BF16)]
            scratch += [pltpu.VMEM((half, half), F32)]
        else:
            in_specs += [flat(half), tall]
            scratch += [pltpu.VMEM((half, width), F32), pltpu.VMEM((half, half), F32)]
        keep_c, send_c, keep_bd, send_bd, *passed = pl.pallas_call(
            lambda *refs, part=part: pair_kernel(part, *refs),
            grid=(steps,),
            in_specs=in_specs,
            out_specs=out_specs,
            out_shape=out_shape,
            scratch_shapes=scratch,
            compiler_params=BIG,
            cost_estimate=pl.CostEstimate(flops=3 * depth * width * width, bytes_accessed=4 * depth * width, transcendentals=0),
            name=f"pair_tiles_{part}",
        )(pos, turned, y_raw[part], w_raw[part], stat_chunked, y_stat, w_stat, *passed)
        send_bd, send_c, *before = lax.optimization_barrier((send_bd, send_c, *before))
        arrived += before
        before = [send(send_bd, across_active), send(send_c, across)]
        keeps.append((keep_bd, keep_c))
    arrived += before

    held, sides = [], []
    for part, (keep_bd, keep_c) in enumerate(keeps):
        sent = jax.ShapeDtypeStruct((strip, width + half * len(D_BLOCKS[part])), sent_as[part])
        held_b, held_c, to_y, to_z = pl.pallas_call(
            lambda *refs, part=part: strips_kernel(part, *refs),
            in_specs=[SMEM] + [VMEM] * 4,
            out_specs=[VMEM] * 4,
            out_shape=[jax.ShapeDtypeStruct((2, strip, half), F32)] * 2 + [sent] * 2,
            name=f"strips_{part}",
        )(pos, keep_c, arrived[2 + 2 * part], keep_bd, arrived[1 + 2 * part])
        held += [held_b, held_c]
        sides += [send(to_y, y_cross), send(to_z, z_cross)]

    four = jax.ShapeDtypeStruct((4, strip, width), F32)
    mine, sib = pl.pallas_call(
        combine_kernel,
        in_specs=[SMEM] + [VMEM] * 10,
        out_specs=[VMEM] * 2,
        out_shape=[four] * 2,
        name="combine",
    )(pos, *held, *sides, diag_keep, arrived[0])

    return pl.pallas_call(
        finish_kernel,
        in_specs=[SMEM, SMEM, VMEM, VMEM],
        out_specs=[VMEM, VMEM],
        out_shape=[jax.ShapeDtypeStruct((1, SLOTS, strip, width), BF16),
                   jax.ShapeDtypeStruct((1, 2, strip, width), BF16)],
        name="finish",
    )(pos, pair_offsets, mine, send(sib, sibling))


def solution(mesh):
    in_specs = (P("samp", "var"), P("var", None), P("var"))
    out_specs = (P("var", None, "samp", None), P("var", None, "samp", None))
    return jax.shard_map(body, mesh=mesh, in_specs=in_specs, out_specs=out_specs, check_vma=False)
```

profile of v0, /device:TPU:0, one launch (start us, length us, event | category | flops | bytes accessed | tf_op | source)
XLA Modules:
  0.0 109.9 jit_solution(5222131947532789644)
XLA Ops:
  0.6 5.9 %chunks_and_local_stats.1 = (bf16[4096,256]{1,0:T(8,128)(2,1)}, bf16[4096,256]{1,0:T(8,128)(2,1)}, f32[2,512]{1,0:T(2,128)}) custom-call(bf16[4096,512]{1,0:T(8,128)(2,1)} %x_ref.1), custom_call_target="tpu_custom_call" | custom-call | flops 10485760 | bytes 8388608 | tf_op jit(solution)/shard_map/chunks_and_local_stats/pallas_call | solution.py:310
  6.5 1.3 %collective-permute-start.3 = (bf16[4096,256]{1,0:T(8,128)(2,1)}, bf16[4096,256]{1,0:T(8,128)(2,1)S(1)}, u32[]{:S(2)}, u32[]{:S(2)}) collective-permute-start(bf16[4096,256]{1,0:T(8,128)(2,1)} %get-tuple-element.44), channel_id=1, source_target_pairs={{1,5},{3,7},{4,0},{6,2},{9,13},{11,15},{12,8},{14,10},{17,21},{19,... | collective-permute-start | bytes 6291464 | tf_op jit(solution)/shard_map/ppermute | solution.py:300
  7.8 1.3 %collective-permute-start.4 = (bf16[4096,256]{1,0:T(8,128)(2,1)}, bf16[4096,256]{1,0:T(8,128)(2,1)}, u32[]{:S(2)}, u32[]{:S(2)}) collective-permute-start(bf16[4096,256]{1,0:T(8,128)(2,1)} %get-tuple-element.44), channel_id=1, source_target_pairs={{1,9},{3,11},{5,13},{7,15},{8,0},{9,17},{10,2},{11,19},{12,4},{13,... | collective-permute-start | bytes 6291464 | tf_op jit(solution)/shard_map/ppermute | solution.py:300
  9.1 6.6 %collective-permute-start = (f32[2,512]{1,0:T(2,128)}, f32[2,512]{1,0:T(2,128)S(1)}, u32[]{:S(2)}, u32[]{:S(2)}) collective-permute-start(f32[2,512]{1,0:T(2,128)} %get-tuple-element.39.own_ref), channel_id=1, source_target_pairs={{0,1},{1,0},{2,3},{3,2},{4,5},{5,4},{6,7},{7,6},{8,9},{9,8},{10,11... | collective-permute-start | bytes 12296 | tf_op jit(solution)/shard_map/ppermute | solution.py:300
  15.7 1.5 %collective-permute-start.1 = (f32[2,512]{1,0:T(2,128)}, f32[2,512]{1,0:T(2,128)S(1)}, u32[]{:S(2)}, u32[]{:S(2)}) collective-permute-start(f32[2,512]{1,0:T(2,128)} %get-tuple-element.39.own_ref), channel_id=1, source_target_pairs={{0,2},{1,3},{2,0},{3,1},{4,6},{5,7},{6,4},{7,5},{8,10},{9,11},{10,... | collective-permute-start | bytes 12296 | tf_op jit(solution)/shard_map/ppermute | solution.py:300
  17.2 0.0 collective-permute-start.2
  17.9 0.6 stack.27.pos_ref.refs_0_
  18.5 1.1 collective-permute-done.1.far_ref
  19.5 0.9 collective-permute-done.2.cross_ref
  20.5 0.6 copy-done.16
  21.0 1.4 %stats.1 = (f32[4,512]{1,0:T(4,128)}, f32[4,512]{1,0:T(4,128)}) custom-call(s32[6]{0:T(128)} %stack.27.pos_ref.refs_0_, s32[1]{0:T(128)S(6)} %copy.5.live_ref, s32[1,3]{1,0:T(1,128)} %offsets_ref.3, f32[2,512]{1,0:T(2,128)} %get-tuple-element.39.own_ref, f32[2,512]{1,0:T(2,128)} %copy-done.14, f32[2,512]{1,0:T(2,128)} %copy-done.15, f32[2,512]{1,0:T(2,128)} %copy-done.16), custom_call_target="tpu_custom_call" | custom-call | tf_op jit(solution)/shard_map/stats/pallas_call | solution.py:323
  22.5 1.3 %collective-permute-start.7 = (bf16[4096,256]{1,0:T(8,128)(2,1)}, bf16[4096,256]{1,0:T(8,128)(2,1)S(1)}, u32[]{:S(2)}, u32[]{:S(2)}) collective-permute-start(bf16[4096,256]{1,0:T(8,128)(2,1)} %get-tuple-element.47), channel_id=1, source_target_pairs={{1,5},{3,7},{4,0},{6,2},{9,13},{11,15},{12,8},{14,10},{17,21},{19,... | collective-permute-start | bytes 6291464 | tf_op jit(solution)/shard_map/ppermute | solution.py:300
  23.8 1.3 %collective-permute-start.8 = (bf16[4096,256]{1,0:T(8,128)(2,1)}, bf16[4096,256]{1,0:T(8,128)(2,1)S(1)}, u32[]{:S(2)}, u32[]{:S(2)}) collective-permute-start(bf16[4096,256]{1,0:T(8,128)(2,1)} %get-tuple-element.47), channel_id=1, source_target_pairs={{1,9},{3,11},{5,13},{7,15},{8,0},{9,17},{10,2},{11,19},{12,4},{13,... | collective-permute-start | bytes 6291464 | tf_op jit(solution)/shard_map/ppermute | solution.py:300
  25.1 3.0 %collective-permute-start.5 = (f32[4,512]{1,0:T(4,128)}, f32[4,512]{1,0:T(4,128)S(1)}, u32[]{:S(2)}, u32[]{:S(2)}) collective-permute-start(f32[4,512]{1,0:T(4,128)} %get-tuple-element.45.refs_4_), channel_id=1, source_target_pairs={{0,5},{2,7},{5,0},{7,2},{8,13},{10,15},{13,8},{15,10},{16,21},{18,... | collective-permute-start | bytes 24584 | tf_op jit(solution)/shard_map/ppermute | solution.py:300
  28.1 2.4 %collective-permute-done.5.refs_5_ = f32[4,512]{1,0:T(4,128)S(1)} collective-permute-done((f32[4,512]{1,0:T(4,128)}, f32[4,512]{1,0:T(4,128)S(1)}, u32[]{:S(2)}, u32[]{:S(2)}) %collective-permute-start.5) | collective-permute-done | bytes 8224 | tf_op jit(solution)/shard_map/ppermute | solution.py:300
  30.4 1.9 %collective-permute-start.6 = (f32[4,512]{1,0:T(4,128)}, f32[4,512]{1,0:T(4,128)S(1)}, u32[]{:S(2)}, u32[]{:S(2)}) collective-permute-start(f32[4,512]{1,0:T(4,128)} %get-tuple-element.45.refs_4_), channel_id=1, source_target_pairs={{0,9},{2,11},{4,13},{6,15},{8,17},{9,0},{10,19},{11,2},{12,21},{13... | collective-permute-start | bytes 24584 | tf_op jit(solution)/shard_map/ppermute | solution.py:300
  32.3 6.9 %own_tile.1 = (bf16[512,4096]{1,0:T(8,128)(2,1)}, f32[256,512]{1,0:T(8,128)}, f32[256,512]{1,0:T(8,128)}) custom-call(s32[6]{0:T(128)} %stack.27.pos_ref.refs_0_, bf16[4096,512]{1,0:T(8,128)(2,1)} %x_ref.1, f32[4,512]{1,0:T(4,128)} %get-tuple-element.42.stat_ref), custom_call_target="tpu_custom_call" | custom-call | flops 2147483648 | bytes 8388608 | tf_op jit(solution)/shard_map/own_tile/pallas_call | solution.py:338
  39.3 0.0 copy-start.13
  39.3 1.2 %collective-permute-start.9 = (f32[256,512]{1,0:T(8,128)}, f32[256,512]{1,0:T(8,128)S(1)}, u32[]{:S(2)}, u32[]{:S(2)}) collective-permute-start(f32[256,512]{1,0:T(8,128)} %get-tuple-element.54), channel_id=1, source_target_pairs={{0,2},{1,3},{2,0},{3,1},{4,6},{5,7},{6,4},{7,5},{8,10},{9,11},{10,... | collective-permute-start | bytes 1572872 | tf_op jit(solution)/shard_map/ppermute | solution.py:300
  40.5 1.3 %copy-done.17 = bf16[4096,256]{1,0:T(8,128)(2,1)} copy-done((bf16[4096,256]{1,0:T(8,128)(2,1)}, bf16[4096,256]{1,0:T(8,128)(2,1)S(1)}, u32[]{:S(2)}) %copy-start.17) | copy-done | bytes 2097176
  41.8 9.1 %pair_tiles_0.1 = (f32[6,128,128]{2,1,0:T(8,128)}, f32[6,128,128]{2,1,0:T(8,128)}, f32[9,128,128]{2,1,0:T(8,128)}, f32[9,128,128]{2,1,0:T(8,128)}, bf16[256,4096]{1,0:T(8,128)(2,1)}, /*index=5*/bf16[4096,256]{1,0:T(8,128)(2,1)}) custom-call(s32[6]{0:T(128)} %stack.27.pos_ref.refs_0_, bf16[512,4096]{1,0:T(8,128)(2,1)} %get-tuple-element.43.refs_1_, ...), custom_call_target="tpu_custom_call" | custom-call | flops 3221225472 | bytes 8388608 | tf_op jit(solution)/shard_map/pair_tiles_0/pallas_call | solution.py:365
  50.9 2.8 %collective-permute-start.10 = (f32[9,128,128]{2,1,0:T(8,128)}, f32[9,128,128]{2,1,0:T(8,128)S(1)}, u32[]{:S(2)}, u32[]{:S(2)}) collective-permute-start(f32[9,128,128]{2,1,0:T(8,128)} %get-tuple-element.55), channel_id=1, source_target_pairs={{0,2},{2,0},{5,7},{7,5},{8,10},{10,8},{13,15},{15,13},{16,18},{18,... | collective-permute-start | bytes 1769480 | tf_op jit(solution)/shard_map/ppermute | solution.py:300
  53.7 1.2 %collective-permute-start.11 = (f32[6,128,128]{2,1,0:T(8,128)}, f32[6,128,128]{2,1,0:T(8,128)S(1)}, u32[]{:S(2)}, u32[]{:S(2)}) collective-permute-start(f32[6,128,128]{2,1,0:T(8,128)} %get-tuple-element.56), channel_id=1, source_target_pairs={{0,2},{1,3},{2,0},{3,1},{4,6},{5,7},{6,4},{7,5},{8,10},{9,11},{10,... | collective-permute-start | bytes 1179656 | tf_op jit(solution)/shard_map/ppermute | solution.py:300
  54.9 2.7 %collective-permute-done.7.refs_2_ = bf16[4096,256]{1,0:T(8,128)(2,1)S(1)} collective-permute-done((bf16[4096,256]{1,0:T(8,128)(2,1)}, bf16[4096,256]{1,0:T(8,128)(2,1)S(1)}, u32[]{:S(2)}, u32[]{:S(2)}) %collective-permute-start.7) | collective-permute-done | bytes 2097184 | tf_op jit(solution)/shard_map/ppermute | solution.py:300
  57.6 2.0 %collective-permute-done.8.refs_3_ = bf16[4096,256]{1,0:T(8,128)(2,1)S(1)} collective-permute-done((bf16[4096,256]{1,0:T(8,128)(2,1)}, bf16[4096,256]{1,0:T(8,128)(2,1)S(1)}, u32[]{:S(2)}, u32[]{:S(2)}) %collective-permute-start.8) | collective-permute-done | bytes 2097184 | tf_op jit(solution)/shard_map/ppermute | solution.py:300
  59.5 1.4 %copy-done.1 = bf16[4096,256]{1,0:T(8,128)(2,1)} copy-done((bf16[4096,256]{1,0:T(8,128)(2,1)}, bf16[4096,256]{1,0:T(8,128)(2,1)S(1)}, u32[]{:S(2)}) %copy-start.1) | copy-done | bytes 2097176
  60.9 10.0 %pair_tiles_1.1 = (f32[6,128,128]{2,1,0:T(8,128)}, bf16[6,128,128]{2,1,0:T(8,128)(2,1)}, f32[15,128,128]{2,1,0:T(8,128)}, bf16[15,128,128]{2,1,0:T(8,128)(2,1)}) custom-call(s32[6]{0:T(128)} %stack.27.pos_ref.refs_0_, bf16[512,4096]{1,0:T(8,128)(2,1)} %get-tuple-element.43.refs_1_, bf16[4096,256]{1,0:T(8,128)(2,1)} %copy-done, bf16[4096,256]{1,0:T(8,128)(2,1)} %copy-done.1, ...), custom_call_target="tpu_custom_call" | custom-call | flops 3221225472 | bytes 8388608 | tf_op jit(solution)/shard_map/pair_tiles_1/pallas_call | solution.py:365
  71.0 3.8 %collective-permute-start.13 = (bf16[15,128,128]{2,1,0:T(8,128)(2,1)}, bf16[15,128,128]{2,1,0:T(8,128)(2,1)S(1)}, u32[]{:S(2)}, u32[]{:S(2)}) collective-permute-start(bf16[15,128,128]{2,1,0:T(8,128)(2,1)} %get-tuple-element.65), channel_id=1, source_target_pairs={{0,2},{2,0},{5,7},{7,5},{8,10},{10,8},{13,15},{15,13},{16,18},{18,... | collective-permute-start | bytes 1474568 | tf_op jit(solution)/shard_map/ppermute | solution.py:300
  74.8 0.2 collective-permute-start.12
  75.0 2.9 %strips_0.1 = (f32[2,128,256]{2,1,0:T(8,128)}, f32[2,128,256]{2,1,0:T(8,128)}, f32[128,768]{1,0:T(8,128)}, f32[128,768]{1,0:T(8,128)}) custom-call(s32[6]{0:T(128)} %stack.27.pos_ref.refs_0_, f32[6,128,128]{2,1,0:T(8,128)} %get-tuple-element.46.refs_1_, f32[6,128,128]{2,1,0:T(8,128)} %copy-done.6, f32[9,128,128]{2,1,0:T(8,128)} %get-tuple-element.58.refs_3_, ...), custom_call_target="tpu_custom_call" | custom-call | tf_op jit(solution)/shard_map/strips_0/pallas_call | solution.py:385
  77.9 1.9 %collective-permute-start.14 = (f32[128,768]{1,0:T(8,128)}, f32[128,768]{1,0:T(8,128)S(1)}, u32[]{:S(2)}, u32[]{:S(2)}) collective-permute-start(f32[128,768]{1,0:T(8,128)} %get-tuple-element.68), channel_id=1, source_target_pairs={{0,5},{2,7},{5,0},{7,2},{8,13},{10,15},{13,8},{15,10},{16,21},{18,... | collective-permute-start | bytes 1179656 | tf_op jit(solution)/shard_map/ppermute | solution.py:300
  79.8 1.9 %collective-permute-start.15 = (f32[128,768]{1,0:T(8,128)}, f32[128,768]{1,0:T(8,128)S(1)}, u32[]{:S(2)}, u32[]{:S(2)}) collective-permute-start(f32[128,768]{1,0:T(8,128)} %get-tuple-element.69), channel_id=1, source_target_pairs={{0,9},{2,11},{4,13},{6,15},{8,17},{9,0},{10,19},{11,2},{12,21},{13... | collective-permute-start | bytes 1179656 | tf_op jit(solution)/shard_map/ppermute | solution.py:300
  81.7 2.3 %collective-permute-done.12.refs_2_ = bf16[6,128,128]{2,1,0:T(8,128)(2,1)S(1)} collective-permute-done((bf16[6,128,128]{2,1,0:T(8,128)(2,1)}, bf16[6,128,128]{2,1,0:T(8,128)(2,1)S(1)}, u32[]{:S(2)}, u32[]{:S(2)}) %collective-permute-start.12) | collective-permute-done | bytes 196640 | tf_op jit(solution)/shard_map/ppermute | solution.py:300
  84.0 0.0 collective-permute-done.13.refs_4_
  84.0 0.7 copy-done.11
  84.7 0.2 copy-done.5
  84.9 2.9 %strips_1.1 = (f32[2,128,256]{2,1,0:T(8,128)}, f32[2,128,256]{2,1,0:T(8,128)}, bf16[128,1280]{1,0:T(8,128)(2,1)}, bf16[128,1280]{1,0:T(8,128)(2,1)}) custom-call(s32[6]{0:T(128)} %stack.27.pos_ref.refs_0_, f32[6,128,128]{2,1,0:T(8,128)} %get-tuple-element.62.refs_1_, bf16[6,128,128]{2,1,0:T(8,128)(2,1)} %copy-done.11, ...), custom_call_target="tpu_custom_call" | custom-call | tf_op jit(solution)/shard_map/strips_1/pallas_call | solution.py:385
  87.8 2.6 %collective-permute-start.16 = (bf16[128,1280]{1,0:T(8,128)(2,1)}, bf16[128,1280]{1,0:T(8,128)(2,1)S(1)}, u32[]{:S(2)}, u32[]{:S(2)}) collective-permute-start(bf16[128,1280]{1,0:T(8,128)(2,1)} %get-tuple-element.70), channel_id=1, source_target_pairs={{0,5},{2,7},{5,0},{7,2},{8,13},{10,15},{13,8},{15,10},{16,21},{18,... | collective-permute-start | bytes 983048 | tf_op jit(solution)/shard_map/ppermute | solution.py:300
  90.5 1.9 %collective-permute-start.17 = (bf16[128,1280]{1,0:T(8,128)(2,1)}, bf16[128,1280]{1,0:T(8,128)(2,1)S(1)}, u32[]{:S(2)}, u32[]{:S(2)}) collective-permute-start(bf16[128,1280]{1,0:T(8,128)(2,1)} %get-tuple-element.71), channel_id=1, source_target_pairs={{0,9},{2,11},{4,13},{6,15},{8,17},{9,0},{10,19},{11,2},{12,21},{13... | collective-permute-start | bytes 983048 | tf_op jit(solution)/shard_map/ppermute | solution.py:300
  92.4 0.0 collective-permute-done.14.y_0
  92.4 0.0 copy-start.7
  92.4 4.0 %collective-permute-done.16.y_1 = bf16[128,1280]{1,0:T(8,128)(2,1)S(1)} collective-permute-done((bf16[128,1280]{1,0:T(8,128)(2,1)}, bf16[128,1280]{1,0:T(8,128)(2,1)S(1)}, u32[]{:S(2)}, u32[]{:S(2)}) %collective-permute-start.16) | collective-permute-done | bytes 327712 | tf_op jit(solution)/shard_map/ppermute | solution.py:300
  96.4 2.7 %collective-permute-done.17.z_1 = bf16[128,1280]{1,0:T(8,128)(2,1)S(1)} collective-permute-done((bf16[128,1280]{1,0:T(8,128)(2,1)}, bf16[128,1280]{1,0:T(8,128)(2,1)S(1)}, u32[]{:S(2)}, u32[]{:S(2)}) %collective-permute-start.17) | collective-permute-done | bytes 327712 | tf_op jit(solution)/shard_map/ppermute | solution.py:300
  99.1 0.7 copy-done.10
  99.8 3.6 %combine.1 = (f32[4,128,512]{2,1,0:T(8,128)}, f32[4,128,512]{2,1,0:T(8,128)}) custom-call(s32[6]{0:T(128)} %stack.27.pos_ref.refs_0_, f32[2,128,256]{2,1,0:T(8,128)} %get-tuple-element.60.held_b0, f32[2,128,256]{2,1,0:T(8,128)} %get-tuple-element.61.held_c0, f32[2,128,256]{2,1,0:T(8,128)} %get-tuple-element.66.held_b1, ...), custom_call_target="tpu_custom_call" | custom-call | tf_op jit(solution)/shard_map/combine/pallas_call | solution.py:396
  103.4 2.9 %collective-permute-done.18.sib = f32[4,128,512]{2,1,0:T(8,128)S(1)} collective-permute-done((f32[4,128,512]{2,1,0:T(8,128)}, f32[4,128,512]{2,1,0:T(8,128)S(1)}, u32[]{:S(2)}, u32[]{:S(2)}) %collective-permute-start.18) | collective-permute-done | bytes 1048608 | tf_op jit(solution)/shard_map/ppermute | solution.py:300
  106.3 1.0 copy-done.2
  107.2 2.6 %finish.1 = (bf16[1,3,128,512]{3,2,1,0:T(8,128)(2,1)}, bf16[1,2,128,512]{3,2,1,0:T(8,128)(2,1)}) custom-call(s32[6]{0:T(128)} %stack.27.pos_ref.refs_0_, s32[1,3]{1,0:T(1,128)} %offsets_ref.3, f32[4,128,512]{2,1,0:T(8,128)} %get-tuple-element.74.mine, f32[4,128,512]{2,1,0:T(8,128)} %copy-done.2), custom_call_target="tpu_custom_call" | custom-call | tf_op jit(solution)/shard_map/finish/pallas_call | solution.py:404
  (36 shorter events, 0.1 us)
Async XLA Ops:
  6.5 33.9 %collective-permute-start.3 = (bf16[4096,256]{1,0:T(8,128)(2,1)}, bf16[4096,256]{1,0:T(8,128)(2,1)S(1)}, u32[]{:S(2)}, u32[]{:S(2)}) collective-permute-start(bf16[4096,256]{1,0:T(8,128)(2,1)} %get-tuple-element.44), channel_id=1, source_target_pairs={{1,5},{3,7},{4,0},{6,2},{9,13},{11,15},{12,8},{14,10},{17,21},{19,... | collective-permute-start | bytes 6291464 | tf_op jit(solution)/shard_map/ppermute | solution.py:300
  7.8 32.7 %collective-permute-start.4 = (bf16[4096,256]{1,0:T(8,128)(2,1)}, bf16[4096,256]{1,0:T(8,128)(2,1)}, u32[]{:S(2)}, u32[]{:S(2)}) collective-permute-start(bf16[4096,256]{1,0:T(8,128)(2,1)} %get-tuple-element.44), channel_id=1, source_target_pairs={{1,9},{3,11},{5,13},{7,15},{8,0},{9,17},{10,2},{11,19},{12,4},{13,... | collective-permute-start | bytes 6291464 | tf_op jit(solution)/shard_map/ppermute | solution.py:300
  9.1 9.3 %collective-permute-start = (f32[2,512]{1,0:T(2,128)}, f32[2,512]{1,0:T(2,128)S(1)}, u32[]{:S(2)}, u32[]{:S(2)}) collective-permute-start(f32[2,512]{1,0:T(2,128)} %get-tuple-element.39.own_ref), channel_id=1, source_target_pairs={{0,1},{1,0},{2,3},{3,2},{4,5},{5,4},{6,7},{7,6},{8,9},{9,8},{10,11... | collective-permute-start | bytes 12296 | tf_op jit(solution)/shard_map/ppermute | solution.py:300
  15.7 3.8 %collective-permute-start.1 = (f32[2,512]{1,0:T(2,128)}, f32[2,512]{1,0:T(2,128)S(1)}, u32[]{:S(2)}, u32[]{:S(2)}) collective-permute-start(f32[2,512]{1,0:T(2,128)} %get-tuple-element.39.own_ref), channel_id=1, source_target_pairs={{0,2},{1,3},{2,0},{3,1},{4,6},{5,7},{6,4},{7,5},{8,10},{9,11},{10,... | collective-permute-start | bytes 12296 | tf_op jit(solution)/shard_map/ppermute | solution.py:300
  17.2 3.2 %collective-permute-start.2 = (f32[2,512]{1,0:T(2,128)}, f32[2,512]{1,0:T(2,128)S(1)}, u32[]{:S(2)}, u32[]{:S(2)}) collective-permute-start(f32[2,512]{1,0:T(2,128)} %get-tuple-element.39.own_ref), channel_id=1, source_target_pairs={{0,3},{1,2},{2,1},{3,0},{4,7},{5,6},{6,5},{7,4},{8,11},{9,10},{10,... | collective-permute-start | bytes 12296 | tf_op jit(solution)/shard_map/ppermute | solution.py:300
  18.5 2.0 %copy-start.14 = (f32[2,512]{1,0:T(2,128)}, f32[2,512]{1,0:T(2,128)S(1)}, u32[]{:S(2)}) copy-start(f32[2,512]{1,0:T(2,128)S(1)} %collective-permute-done.sib_ref) | copy-start | bytes 12292
  19.5 0.9 copy-start.15
  20.5 0.6 copy-start.16
  22.5 35.1 %collective-permute-start.7 = (bf16[4096,256]{1,0:T(8,128)(2,1)}, bf16[4096,256]{1,0:T(8,128)(2,1)S(1)}, u32[]{:S(2)}, u32[]{:S(2)}) collective-permute-start(bf16[4096,256]{1,0:T(8,128)(2,1)} %get-tuple-element.47), channel_id=1, source_target_pairs={{1,5},{3,7},{4,0},{6,2},{9,13},{11,15},{12,8},{14,10},{17,21},{19,... | collective-permute-start | bytes 6291464 | tf_op jit(solution)/shard_map/ppermute | solution.py:300
  23.8 35.8 %collective-permute-start.8 = (bf16[4096,256]{1,0:T(8,128)(2,1)}, bf16[4096,256]{1,0:T(8,128)(2,1)S(1)}, u32[]{:S(2)}, u32[]{:S(2)}) collective-permute-start(bf16[4096,256]{1,0:T(8,128)(2,1)} %get-tuple-element.47), channel_id=1, source_target_pairs={{1,9},{3,11},{5,13},{7,15},{8,0},{9,17},{10,2},{11,19},{12,4},{13,... | collective-permute-start | bytes 6291464 | tf_op jit(solution)/shard_map/ppermute | solution.py:300
  25.1 5.3 %collective-permute-start.5 = (f32[4,512]{1,0:T(4,128)}, f32[4,512]{1,0:T(4,128)S(1)}, u32[]{:S(2)}, u32[]{:S(2)}) collective-permute-start(f32[4,512]{1,0:T(4,128)} %get-tuple-element.45.refs_4_), channel_id=1, source_target_pairs={{0,5},{2,7},{5,0},{7,2},{8,13},{10,15},{13,8},{15,10},{16,21},{18,... | collective-permute-start | bytes 24584 | tf_op jit(solution)/shard_map/ppermute | solution.py:300
  30.4 8.8 %copy-start.12 = (f32[4,512]{1,0:T(4,128)}, f32[4,512]{1,0:T(4,128)S(1)}, u32[]{:S(2)}) copy-start(f32[4,512]{1,0:T(4,128)S(1)} %collective-permute-done.5.refs_5_) | copy-start | bytes 24580
  30.4 8.8 %collective-permute-start.6 = (f32[4,512]{1,0:T(4,128)}, f32[4,512]{1,0:T(4,128)S(1)}, u32[]{:S(2)}, u32[]{:S(2)}) collective-permute-start(f32[4,512]{1,0:T(4,128)} %get-tuple-element.45.refs_4_), channel_id=1, source_target_pairs={{0,9},{2,11},{4,13},{6,15},{8,17},{9,0},{10,19},{11,2},{12,21},{13... | collective-permute-start | bytes 24584 | tf_op jit(solution)/shard_map/ppermute | solution.py:300
  39.3 1.2 %copy-start.13 = (f32[4,512]{1,0:T(4,128)}, f32[4,512]{1,0:T(4,128)S(1)}, u32[]{:S(2)}) copy-start(f32[4,512]{1,0:T(4,128)S(1)} %collective-permute-done.6.refs_6_) | copy-start | bytes 24580
  39.3 11.6 %collective-permute-start.9 = (f32[256,512]{1,0:T(8,128)}, f32[256,512]{1,0:T(8,128)S(1)}, u32[]{:S(2)}, u32[]{:S(2)}) collective-permute-start(f32[256,512]{1,0:T(8,128)} %get-tuple-element.54), channel_id=1, source_target_pairs={{0,2},{1,3},{2,0},{3,1},{4,6},{5,7},{6,4},{7,5},{8,10},{9,11},{10,... | collective-permute-start | bytes 1572872 | tf_op jit(solution)/shard_map/ppermute | solution.py:300
  40.5 1.3 %copy-start.17 = (bf16[4096,256]{1,0:T(8,128)(2,1)}, bf16[4096,256]{1,0:T(8,128)(2,1)S(1)}, u32[]{:S(2)}) copy-start(bf16[4096,256]{1,0:T(8,128)(2,1)S(1)} %collective-permute-done.3.refs_2_) | copy-start | bytes 6291460
  50.9 20.1 %copy-start.4 = (f32[256,512]{1,0:T(8,128)}, f32[256,512]{1,0:T(8,128)S(1)}, u32[]{:S(2)}) copy-start(f32[256,512]{1,0:T(8,128)S(1)} %collective-permute-done.9.diag_got) | copy-start | bytes 1572868
  50.9 20.1 %collective-permute-start.10 = (f32[9,128,128]{2,1,0:T(8,128)}, f32[9,128,128]{2,1,0:T(8,128)S(1)}, u32[]{:S(2)}, u32[]{:S(2)}) collective-permute-start(f32[9,128,128]{2,1,0:T(8,128)} %get-tuple-element.55), channel_id=1, source_target_pairs={{0,2},{2,0},{5,7},{7,5},{8,10},{10,8},{13,15},{15,13},{16,18},{18,... | collective-permute-start | bytes 1769480 | tf_op jit(solution)/shard_map/ppermute | solution.py:300
  53.7 17.3 %collective-permute-start.11 = (f32[6,128,128]{2,1,0:T(8,128)}, f32[6,128,128]{2,1,0:T(8,128)S(1)}, u32[]{:S(2)}, u32[]{:S(2)}) collective-permute-start(f32[6,128,128]{2,1,0:T(8,128)} %get-tuple-element.56), channel_id=1, source_target_pairs={{0,2},{1,3},{2,0},{3,1},{4,6},{5,7},{6,4},{7,5},{8,10},{9,11},{10,... | collective-permute-start | bytes 1179656 | tf_op jit(solution)/shard_map/ppermute | solution.py:300
  57.6 2.0 %copy-start = (bf16[4096,256]{1,0:T(8,128)(2,1)}, bf16[4096,256]{1,0:T(8,128)(2,1)S(1)}, u32[]{:S(2)}) copy-start(bf16[4096,256]{1,0:T(8,128)(2,1)S(1)} %collective-permute-done.7.refs_2_) | copy-start | bytes 6291460
  59.5 1.4 %copy-start.1 = (bf16[4096,256]{1,0:T(8,128)(2,1)}, bf16[4096,256]{1,0:T(8,128)(2,1)S(1)}, u32[]{:S(2)}) copy-start(bf16[4096,256]{1,0:T(8,128)(2,1)S(1)} %collective-permute-done.8.refs_3_) | copy-start | bytes 6291460
  71.0 4.0 %copy-start.6 = (f32[6,128,128]{2,1,0:T(8,128)}, f32[6,128,128]{2,1,0:T(8,128)S(1)}, u32[]{:S(2)}) copy-start(f32[6,128,128]{2,1,0:T(8,128)S(1)} %collective-permute-done.11.refs_2_) | copy-start | bytes 1179652
  71.0 4.0 %copy-start.3 = (f32[9,128,128]{2,1,0:T(8,128)}, f32[9,128,128]{2,1,0:T(8,128)S(1)}, u32[]{:S(2)}) copy-start(f32[9,128,128]{2,1,0:T(8,128)S(1)} %collective-permute-done.10.refs_4_) | copy-start | bytes 1769476
  71.0 13.0 %collective-permute-start.13 = (bf16[15,128,128]{2,1,0:T(8,128)(2,1)}, bf16[15,128,128]{2,1,0:T(8,128)(2,1)S(1)}, u32[]{:S(2)}, u32[]{:S(2)}) collective-permute-start(bf16[15,128,128]{2,1,0:T(8,128)(2,1)} %get-tuple-element.65), channel_id=1, source_target_pairs={{0,2},{2,0},{5,7},{7,5},{8,10},{10,8},{13,15},{15,13},{16,18},{18,... | collective-permute-start | bytes 1474568 | tf_op jit(solution)/shard_map/ppermute | solution.py:300
  74.8 9.2 %collective-permute-start.12 = (bf16[6,128,128]{2,1,0:T(8,128)(2,1)}, bf16[6,128,128]{2,1,0:T(8,128)(2,1)S(1)}, u32[]{:S(2)}, u32[]{:S(2)}) collective-permute-start(bf16[6,128,128]{2,1,0:T(8,128)(2,1)} %get-tuple-element.63), channel_id=1, source_target_pairs={{0,2},{1,3},{2,0},{3,1},{4,6},{5,7},{6,4},{7,5},{8,10},{9,11},{10,... | collective-permute-start | bytes 589832 | tf_op jit(solution)/shard_map/ppermute | solution.py:300
  77.9 14.5 %collective-permute-start.14 = (f32[128,768]{1,0:T(8,128)}, f32[128,768]{1,0:T(8,128)S(1)}, u32[]{:S(2)}, u32[]{:S(2)}) collective-permute-start(f32[128,768]{1,0:T(8,128)} %get-tuple-element.68), channel_id=1, source_target_pairs={{0,5},{2,7},{5,0},{7,2},{8,13},{10,15},{13,8},{15,10},{16,21},{18,... | collective-permute-start | bytes 1179656 | tf_op jit(solution)/shard_map/ppermute | solution.py:300
  79.8 12.6 %collective-permute-start.15 = (f32[128,768]{1,0:T(8,128)}, f32[128,768]{1,0:T(8,128)S(1)}, u32[]{:S(2)}, u32[]{:S(2)}) collective-permute-start(f32[128,768]{1,0:T(8,128)} %get-tuple-element.69), channel_id=1, source_target_pairs={{0,9},{2,11},{4,13},{6,15},{8,17},{9,0},{10,19},{11,2},{12,21},{13... | collective-permute-start | bytes 1179656 | tf_op jit(solution)/shard_map/ppermute | solution.py:300
  84.0 0.7 copy-start.11
  84.0 0.8 copy-start.5
  87.8 8.6 %collective-permute-start.16 = (bf16[128,1280]{1,0:T(8,128)(2,1)}, bf16[128,1280]{1,0:T(8,128)(2,1)S(1)}, u32[]{:S(2)}, u32[]{:S(2)}) collective-permute-start(bf16[128,1280]{1,0:T(8,128)(2,1)} %get-tuple-element.70), channel_id=1, source_target_pairs={{0,5},{2,7},{5,0},{7,2},{8,13},{10,15},{13,8},{15,10},{16,21},{18,... | collective-permute-start | bytes 983048 | tf_op jit(solution)/shard_map/ppermute | solution.py:300
  90.5 8.6 %collective-permute-start.17 = (bf16[128,1280]{1,0:T(8,128)(2,1)}, bf16[128,1280]{1,0:T(8,128)(2,1)S(1)}, u32[]{:S(2)}, u32[]{:S(2)}) collective-permute-start(bf16[128,1280]{1,0:T(8,128)(2,1)} %get-tuple-element.71), channel_id=1, source_target_pairs={{0,9},{2,11},{4,13},{6,15},{8,17},{9,0},{10,19},{11,2},{12,21},{13... | collective-permute-start | bytes 983048 | tf_op jit(solution)/shard_map/ppermute | solution.py:300
  92.4 6.7 %copy-start.7 = (f32[128,768]{1,0:T(8,128)}, f32[128,768]{1,0:T(8,128)S(1)}, u32[]{:S(2)}) copy-start(f32[128,768]{1,0:T(8,128)S(1)} %collective-permute-done.14.y_0) | copy-start | bytes 1179652
  92.4 6.7 %copy-start.8 = (f32[128,768]{1,0:T(8,128)}, f32[128,768]{1,0:T(8,128)S(1)}, u32[]{:S(2)}) copy-start(f32[128,768]{1,0:T(8,128)S(1)} %collective-permute-done.15.z_0) | copy-start | bytes 1179652
  96.4 2.7 %copy-start.9 = (bf16[128,1280]{1,0:T(8,128)(2,1)}, bf16[128,1280]{1,0:T(8,128)(2,1)S(1)}, u32[]{:S(2)}) copy-start(bf16[128,1280]{1,0:T(8,128)(2,1)S(1)} %collective-permute-done.16.y_1) | copy-start | bytes 983044
  99.1 0.8 copy-start.10
  103.4 2.9 %collective-permute-start.18 = (f32[4,128,512]{2,1,0:T(8,128)}, f32[4,128,512]{2,1,0:T(8,128)S(1)}, u32[]{:S(2)}, u32[]{:S(2)}) collective-permute-start(f32[4,128,512]{2,1,0:T(8,128)} %get-tuple-element.75), channel_id=1, source_target_pairs={{0,1},{1,0},{2,3},{3,2},{4,5},{5,4},{6,7},{7,6},{8,9},{9,8},{10,11... | collective-permute-start | bytes 3145736 | tf_op jit(solution)/shard_map/ppermute | solution.py:300
  106.3 1.0 copy-start.2
where the time goes:
time: 111 us; the launch traced here: 110 us
  Pallas kernels  45.4 us (41%)
  starting transfers between devices  35.7 us (32%)
  waiting for transfers between devices  20.8 us (19%)
  local copies, waits for them, and re-layouts  6.47 us (6%)
  between operations  1.52 us (1%)
    ppermute x19, starting transfers between devices, send(): return lax.ppermute(value, AXES, pairs)  35.7 us
    ppermute x19, waiting for transfers between devices, send(): return lax.ppermute(value, AXES, pairs)  20.8 us
    pallas_call x2, Pallas kernels, body(): pl.pallas_call(lambda *refs, part=part: pair_kernel(part, *refs), grid=(s...  19.1 us
    pallas_call x1, Pallas kernels, body(): pl.pallas_call(own_kernel, grid=(steps,), in_specs=[SMEM, wide, whole(4,...  6.92 us
    pallas_call x1, Pallas kernels, body(): pl.pallas_call(lambda *refs: first_kernel(steps, *refs), grid=(steps,), i...  5.92 us
    unnamed x36, local copies, waits for them, and re-layouts  5.86 us
    pallas_call x2, Pallas kernels, body(): pl.pallas_call(lambda *refs, part=part: strips_kernel(part, *refs), in_sp...  5.79 us
    pallas_call x1, Pallas kernels, body(): pl.pallas_call(combine_kernel, in_specs=[SMEM] + [VMEM] * 10, out_specs=[...  3.56 us
  transfers between devices with their start and end apart: 19, of which 9 were waited for; matrix products, arithmetic and copies ran while one was open for 1% of the time, Pallas kernels for 30%

commit v1 on v0

--- a/solution.py
+++ b/solution.py
@@ -11,7 +11,8 @@
 BF16 = jnp.bfloat16
 VMEM = pl.BlockSpec(memory_space=pltpu.VMEM)
 SMEM = pl.BlockSpec(memory_space=pltpu.SMEM)
-BIG = pltpu.CompilerParams(vmem_limit_bytes=56 << 20)
+SOME = pltpu.CompilerParams(vmem_limit_bytes=24 << 20)
+MOST = pltpu.CompilerParams(vmem_limit_bytes=58 << 20)
 D_BLOCKS = {0: [(0, 0)], 1: [(0, 1), (1, 0), (1, 1)]}
 
 
@@ -23,15 +24,27 @@
     return ((raw.astype(F32) - stat_ref[0:1, :]) * stat_ref[1:2, :]).astype(BF16)
 
 
-def first_kernel(steps, x_ref, chunk_0, chunk_1, out_ref, center, total, square):
+def cut_kernel(x_ref, out_ref, sems):
+    strip = out_ref.shape[1] // 2
+    copies = [pltpu.make_async_copy(x_ref.at[:, pl.ds(2 * half * strip, strip)],
+                                    out_ref.at[:, pl.ds(half * strip, strip)], sems.at[half]) for half in range(2)]
+    for copy in copies:
+        copy.start()
+    for copy in copies:
+        copy.wait()
+
+
+def first_kernel(steps, x_ref, upper_ref, lower_ref, out_ref, center, total, square):
     step = pl.program_id(0)
     rows, width = x_ref.shape
-    strip = chunk_0.shape[1] // 2
+    strip = upper_ref.shape[1] // 2
     group = min(64, rows)
-    for part, out in enumerate((chunk_0, chunk_1)):
-        for half in range(2):
-            start = (2 * half + part) * strip
-            out[:, half * strip:(half + 1) * strip] = x_ref[:, start:start + strip]
+    for first, out in ((True, upper_ref), (False, lower_ref)):
+        @pl.when((step < steps // 2) == first)
+        def _():
+            for half in range(2):
+                start = (2 * half + 1) * strip
+                out[:, half * strip:(half + 1) * strip] = x_ref[:, start:start + strip]
 
     @pl.when(step == 0)
     def _():
@@ -118,27 +131,30 @@
                 index += 1
 
 
-def pair_kernel(chunk, *refs):
+def pair_kernel(stage, *refs):
     (pos_ref, turned_ref, y_ref, w_ref, stat_ref, ystat_ref, wstat_ref), refs = refs[:7], refs[7:]
-    if chunk == 0:
-        keep_c, send_c, keep_bd, send_bd, yt_out, w_out, acc_b, acc_c, acc_d = refs
+    if stage == 0:
+        (keep_c, send_c, keep_bd, send_bd, yt_out, w_out), accs = refs[:6], refs[6:]
+    elif stage == 1:
+        (yt_old, w_old), accs = refs[:2], refs[2:]
     else:
-        yt_old, w_old, keep_c, send_c, keep_bd, send_bd, acc_b, acc_c, acc_d, acc_e = refs
+        (yt_old, w_old), olds, (keep_c, send_c, keep_bd, send_bd), accs = refs[:2], refs[2:6], refs[6:10], refs[10:]
+    acc_b, acc_c, acc_d = accs[:3]
     step = pl.program_id(0)
     last = pl.num_programs(0) - 1
     x = pos_ref[0]
     active = pos_ref[1] == 1
-    size = keep_c.shape[-1]
+    size = y_ref.shape[1] // 2
 
     @pl.when(step == 0)
     def _():
-        for acc in (acc_b, acc_c, acc_d) + (() if chunk == 0 else (acc_e,)):
-            acc[...] = jnp.zeros_like(acc)
+        for index, acc in enumerate(accs):
+            acc[...] = olds[index][...] if stage == 2 else jnp.zeros_like(acc)
 
     zt = turned_ref[...]
     w = standardized(w_ref[...], wstat_ref)
     acc_c[...] += dot(zt, w)
-    if chunk == 0:
+    if stage == 0:
         w_out[...] = w
 
     @pl.when(active)
@@ -146,13 +162,16 @@
         y = standardized(y_ref[...], ystat_ref)
         yt = y.T
         acc_b[...] += dot(zt, y)
-        if chunk == 0:
+        if stage == 0:
             yt_out[...] = yt
             acc_d[...] += dot(yt, w)
         else:
-            acc_e[...] += dot(yt_old[...], w)
+            accs[3][...] += dot(yt_old[...], w)
             acc_d[:, :2 * size] += dot(yt, w_old[...])
             acc_d[:, 2 * size:] += dot(yt, w)
+
+    if stage == 1:
+        return
 
     @pl.when(step == last)
     def _():
@@ -167,9 +186,10 @@
             put_blocks(x, acc_b, 0, keep_bd, send_bd, 0, 2)
             scale = jnp.where(first, ystat_ref[2:3, :], wstat_ref[2:3, :]) * share
             acc_d[:, :2 * size] *= scale
-            if chunk == 0:
+            if stage == 0:
                 put_blocks(x, acc_d, 0, keep_bd, send_bd, 6, 1)
             else:
+                acc_e = accs[3]
                 acc_d[:, 2 * size:] *= scale
                 acc_e[...] *= scale
                 put_blocks(x, acc_e, 0, keep_bd, send_bd, 6, 1)
@@ -307,18 +327,29 @@
     flat = lambda rows: pl.BlockSpec((rows, step_rows), lambda k: (0, k))
     whole = lambda *shape: pl.BlockSpec(shape, lambda k: (0,) * len(shape))
 
-    chunk_0, chunk_1, local = pl.pallas_call(
+    chunk_0 = pl.pallas_call(
+        cut_kernel,
+        in_specs=[pl.BlockSpec(memory_space=pl.ANY)],
+        out_specs=pl.BlockSpec(memory_space=pl.ANY),
+        out_shape=jax.ShapeDtypeStruct((depth, half), BF16),
+        scratch_shapes=[pltpu.SemaphoreType.DMA((2,))],
+        compiler_params=MOST,
+        name="first_chunk",
+    )(dosage)
+    w_raw, y_raw = [send(chunk_0, z_main)], [send(chunk_0, y_main)]
+    dosage, chunk_0 = lax.optimization_barrier((dosage, chunk_0))
+    *pieces, local = pl.pallas_call(
         lambda *refs: first_kernel(steps, *refs),
         grid=(steps,),
         in_specs=[wide],
-        out_specs=[tall, tall, whole(2, width)],
-        out_shape=[jax.ShapeDtypeStruct((depth, half), BF16)] * 2 + [jax.ShapeDtypeStruct((2, width), F32)],
+        out_specs=[pl.BlockSpec((step_rows, half), lambda k: (jnp.minimum(k, steps // 2 - 1), 0)),
+                   pl.BlockSpec((step_rows, half), lambda k: (jnp.maximum(k - steps // 2, 0), 0)), whole(2, width)],
+        out_shape=[jax.ShapeDtypeStruct((depth // 2, half), BF16)] * 2 + [jax.ShapeDtypeStruct((2, width), F32)],
         scratch_shapes=[pltpu.VMEM((1, width), F32)] + [pltpu.VMEM((8, width), F32)] * 2,
-        compiler_params=BIG,
-        cost_estimate=pl.CostEstimate(flops=5 * depth * width, bytes_accessed=4 * depth * width, transcendentals=0),
-        name="chunks_and_local_stats",
+        compiler_params=SOME,
+        cost_estimate=pl.CostEstimate(flops=5 * depth * width, bytes_accessed=3 * depth * width, transcendentals=0),
+        name="second_chunk_and_local_stats",
     )(dosage)
-    w_raw, y_raw = [send(chunk_0, z_main)], [send(chunk_0, y_main)]
     others = [send(local, [(at(a, b), at(a, b ^ flip)) for a, b in everyone]) for flip in (1, 2, 3)]
     stat, stat_chunked = pl.pallas_call(
         stat_kernel,
@@ -327,9 +358,6 @@
         out_shape=[jax.ShapeDtypeStruct((4, width), F32)] * 2,
         name="stats",
     )(pos, live_counts, pair_offsets, local, *others)
-    stat, chunk_1 = lax.optimization_barrier((stat, chunk_1))
-    w_raw.append(send(chunk_1, z_main))
-    y_raw.append(send(chunk_1, y_main))
     z_step = [(a, b, a + 2 if b % 2 == 0 else a - 2) for a, b in everyone]
     z_cross = [(at(a, b), at(t, b ^ 1)) for a, b, t in z_step if 0 <= t < n_var]
     y_cross = [(at(a, b), at(a ^ 1, b ^ 1)) for a, b in everyone if active_on(a, b)]
@@ -342,37 +370,55 @@
         out_specs=[flat(width)] + [whole(half, width)] * 2,
         out_shape=[jax.ShapeDtypeStruct((width, depth), BF16)] + [jax.ShapeDtypeStruct((half, width), F32)] * 2,
         scratch_shapes=[pltpu.VMEM((width, width), F32)],
-        compiler_params=BIG,
+        compiler_params=SOME,
         cost_estimate=pl.CostEstimate(flops=2 * depth * width * width, bytes_accessed=4 * depth * width, transcendentals=0),
         name="own_tile",
     )(pos, dosage, stat)
+    turned, w_stat, y_stat, *pieces = lax.optimization_barrier((turned, w_stat, y_stat, *pieces))
+    for piece in pieces:
+        w_raw.append(send(piece, z_main))
+        y_raw.append(send(piece, y_main))
     diag_across = send(diag_send, across)
     keeps, arrived, passed, before = [], [], [], [diag_across]
     sent_as = (F32, BF16)
-    for part in range(2):
+    for stage in range(3):
+        part = min(stage, 1)
+        here = steps if stage == 0 else steps // 2
+        skip = steps // 2 if stage == 2 else 0
+        lower = lambda rows, skip=skip: pl.BlockSpec((rows, step_rows), lambda k: (0, k + skip))
         n_bd = 6 + 3 * len(D_BLOCKS[part])
-        in_specs = [SMEM, flat(width), tall, tall] + [pl.BlockSpec((4, half), lambda k, part=part: (0, part))] * 3
-        out_specs = [whole(6, strip, strip)] * 2 + [whole(n_bd, strip, strip)] * 2
-        out_shape = [jax.ShapeDtypeStruct((n, strip, strip), kind) for n in (6, n_bd) for kind in (F32, sent_as[part])]
-        scratch = [pltpu.VMEM((width, half), F32)] * 2
-        if part == 0:
+        in_specs = [SMEM, lower(width), tall, tall] + [pl.BlockSpec((4, half), lambda k, part=part: (0, part))] * 3
+        sums = [(width, half), (width, half), (half, half if stage == 0 else width)] + [(half, half)] * part
+        out_specs, out_shape, scratch = [], [], []
+        if stage > 0:
+            in_specs += [lower(half), pl.BlockSpec((step_rows, half), lambda k, skip=skip: (k + skip, 0))]
+        if stage == 2:
+            in_specs += [whole(*shape) for shape in sums]
+        if stage != 1:
+            out_specs += [whole(n, strip, strip) for n in (6, 6, n_bd, n_bd)]
+            out_shape += [jax.ShapeDtypeStruct((n, strip, strip), kind) for n in (6, n_bd) for kind in (F32, sent_as[part])]
+            scratch += [pltpu.VMEM(shape, F32) for shape in sums]
+        else:
+            out_specs += [whole(*shape) for shape in sums]
+            out_shape += [jax.ShapeDtypeStruct(shape, F32) for shape in sums]
+        if stage == 0:
             out_specs += [flat(half), tall]
             out_shape += [jax.ShapeDtypeStruct((half, depth), BF16), jax.ShapeDtypeStruct((depth, half), BF16)]
-            scratch += [pltpu.VMEM((half, half), F32)]
-        else:
-            in_specs += [flat(half), tall]
-            scratch += [pltpu.VMEM((half, width), F32), pltpu.VMEM((half, half), F32)]
-        keep_c, send_c, keep_bd, send_bd, *passed = pl.pallas_call(
-            lambda *refs, part=part: pair_kernel(part, *refs),
-            grid=(steps,),
+        results = pl.pallas_call(
+            lambda *refs, stage=stage: pair_kernel(stage, *refs),
+            grid=(here,),
             in_specs=in_specs,
             out_specs=out_specs,
             out_shape=out_shape,
             scratch_shapes=scratch,
-            compiler_params=BIG,
-            cost_estimate=pl.CostEstimate(flops=3 * depth * width * width, bytes_accessed=4 * depth * width, transcendentals=0),
-            name=f"pair_tiles_{part}",
-        )(pos, turned, y_raw[part], w_raw[part], stat_chunked, y_stat, w_stat, *passed)
+            compiler_params=SOME,
+            cost_estimate=pl.CostEstimate(flops=3 * depth * width * width * here // steps, bytes_accessed=4 * depth * width * here // steps, transcendentals=0),
+            name=f"pair_tiles_{stage}",
+        )(pos, turned, y_raw[stage], w_raw[stage], stat_chunked, y_stat, w_stat, *passed)
+        if stage == 1:
+            passed = [*passed, *results]
+            continue
+        keep_c, send_c, keep_bd, send_bd, *passed = results
         send_bd, send_c, *before = lax.optimization_barrier((send_bd, send_c, *before))
         arrived += before
         before = [send(send_bd, across_active), send(send_c, across)]

time: 111 us -> 179 us (1.61)
  Pallas kernels: 45.4 us -> 98.7 us
  starting transfers between devices: 35.7 us -> 45.1 us
  local copies, waits for them, and re-layouts: 6.47 us -> 10.8 us
    pallas_call x2 -> x4, Pallas kernels: 19.1 us -> 78.7 us  [the longest x1 64.6 us: body(): pl.pallas_call(cut_kernel, in_specs=[pl.BlockSpec(memory_space=pl.ANY)],...]
    ppermute x19 -> x21, starting transfers between devices: 35.7 us -> 45.1 us  [send(): return lax.ppermute(value, AXES, pairs)]
    unnamed x36 -> x54, local copies, waits for them, and re-layouts: 5.86 us -> 10.2 us
    pallas_call x1, Pallas kernels: 5.92 us -> 2.28 us  [body(): pl.pallas_call(lambda *refs: first_kernel(steps, *refs), grid=(steps,), i...]
    pallas_call x1, Pallas kernels: 6.92 us -> 4.3 us  [body(): pl.pallas_call(own_kernel, grid=(steps,), in_specs=[SMEM, wide, whole(4,...]
    ppermute x19 -> x21, waiting for transfers between devices: 20.8 us -> 21 us  [send(): return lax.ppermute(value, AXES, pairs)]
  transfers between devices with their start and end apart: 19 -> 21, of which waited for: 9 -> 8; matrix products, arithmetic and copies ran while one was open for 1% -> 0% of each run, Pallas kernels for 30% -> 16%
where the time goes in v1:
time: 179 us; the launch traced here: 177 us
  Pallas kernels  98.7 us (55%)
  starting transfers between devices  45.1 us (25%)
  waiting for transfers between devices  21 us (12%)
  local copies, waits for them, and re-layouts  10.8 us (6%)
    pallas_call x1, Pallas kernels, body(): pl.pallas_call(cut_kernel, in_specs=[pl.BlockSpec(memory_space=pl.ANY)],...  64.6 us
    ppermute x21, starting transfers between devices, send(): return lax.ppermute(value, AXES, pairs)  45.1 us
    ppermute x21, waiting for transfers between devices, send(): return lax.ppermute(value, AXES, pairs)  21 us
    pallas_call x3, Pallas kernels, body(): pl.pallas_call(lambda *refs, stage=stage: pair_kernel(stage, *refs), grid...  14 us
    unnamed x54, local copies, waits for them, and re-layouts  10.2 us
    pallas_call x2, Pallas kernels, body(): pl.pallas_call(lambda *refs, part=part: strips_kernel(part, *refs), in_sp...  5.83 us
    pallas_call x1, Pallas kernels, body(): pl.pallas_call(own_kernel, grid=(steps,), in_specs=[SMEM, wide, whole(4,...  4.3 us
  transfers between devices with their start and end apart: 21, of which 8 were waited for; matrix products, arithmetic and copies ran while one was open for 0% of the time, Pallas kernels for 16%

profile of v1, /device:TPU:0, one launch (start us, length us, event | category | flops | bytes accessed | tf_op | source)
XLA Modules:
  0.0 177.2 jit_solution(2469075107673193242)
XLA Ops:
  0.6 64.6 %first_chunk.1 = bf16[4096,256]{1,0:T(8,128)(2,1)} custom-call(bf16[4096,512]{1,0:T(8,128)(2,1)} %x_ref.2), custom_call_target="tpu_custom_call" | custom-call | tf_op jit(solution)/shard_map/first_chunk/pallas_call | solution.py:330
  65.3 1.3 collective-permute-start.5
  66.6 1.3 collective-permute-start.6
  67.9 2.3 %second_chunk_and_local_stats.1 = (bf16[2048,256]{1,0:T(8,128)(2,1)S(1)}, bf16[2048,256]{1,0:T(8,128)(2,1)S(1)}, f32[2,512]{1,0:T(2,128)S(1)}) custom-call(bf16[4096,512]{1,0:T(8,128)(2,1)S(1)} %copy-done), custom_call_target="tpu_custom_call" | custom-call | flops 10485760 | bytes 6291456 | tf_op jit(solution)/shard_map/second_chunk_and_local_stats/pallas_call | solution.py:341
  70.2 1.0 copy-done.11
  71.2 7.7 %collective-permute-start = (f32[2,512]{1,0:T(2,128)S(1)}, f32[2,512]{1,0:T(2,128)S(1)}, u32[]{:S(2)}, u32[]{:S(2)}) collective-permute-start(f32[2,512]{1,0:T(2,128)S(1)} %get-tuple-element.48.own_ref), channel_id=1, source_target_pairs={{0,1},{1,0},{2,3},{3,2},{4,5},{5,4},{6,7},{7,6},{8,9},{9,8},{10,11... | collective-permute-start | bytes 12296 | tf_op jit(solution)/shard_map/ppermute | solution.py:320
  78.9 1.5 collective-permute-start.1
  81.0 0.6 stack.27.pos_ref.refs_0_
  81.6 0.9 collective-permute-done.1.far_ref
  82.5 0.9 collective-permute-done.2.cross_ref
  84.0 1.4 stats.1
  85.5 1.9 %collective-permute-start.3 = (f32[4,512]{1,0:T(4,128)}, f32[4,512]{1,0:T(4,128)S(1)}, u32[]{:S(2)}, u32[]{:S(2)}) collective-permute-start(f32[4,512]{1,0:T(4,128)} %get-tuple-element.51.refs_4_), channel_id=1, source_target_pairs={{0,9},{2,11},{4,13},{6,15},{8,17},{9,0},{10,19},{11,2},{12,21},{13... | collective-permute-start | bytes 24584 | tf_op jit(solution)/shard_map/ppermute | solution.py:320
  87.4 1.9 %collective-permute-start.4 = (f32[4,512]{1,0:T(4,128)}, f32[4,512]{1,0:T(4,128)S(1)}, u32[]{:S(2)}, u32[]{:S(2)}) collective-permute-start(f32[4,512]{1,0:T(4,128)} %get-tuple-element.51.refs_4_), channel_id=1, source_target_pairs={{0,5},{2,7},{5,0},{7,2},{8,13},{10,15},{13,8},{15,10},{16,21},{18,... | collective-permute-start | bytes 24584 | tf_op jit(solution)/shard_map/ppermute | solution.py:320
  89.3 2.2 %copy-done.1 = bf16[4096,512]{1,0:T(8,128)(2,1)S(1)} copy-done((bf16[4096,512]{1,0:T(8,128)(2,1)S(1)}, bf16[4096,512]{1,0:T(8,128)(2,1)}, u32[]{:S(2)}) %copy-start.1) | copy-done | bytes 4194328
  92.1 0.7 copy-done.13
  92.8 4.3 %own_tile.1 = (bf16[512,4096]{1,0:T(8,128)(2,1)S(1)}, f32[256,512]{1,0:T(8,128)S(1)}, f32[256,512]{1,0:T(8,128)S(1)}) custom-call(s32[6]{0:T(128)S(1)} %copy-done.8, bf16[4096,512]{1,0:T(8,128)(2,1)S(1)} %copy-done.1, f32[4,512]{1,0:T(4,128)S(1)} %copy-done.13), custom_call_target="tpu_custom_call" | custom-call | flops 2147483648 | bytes 8388608 | tf_op jit(solution)/shard_map/own_tile/pallas_call | solution.py:366
  97.1 0.8 copy-done.4
  97.9 1.3 collective-permute-start.10
  99.2 1.3 collective-permute-start.9
  100.5 1.3 collective-permute-start.7
  101.9 1.3 collective-permute-start.8
  103.2 1.2 collective-permute-start.11
  104.4 6.5 %pair_tiles_0.1 = (f32[6,128,128]{2,1,0:T(8,128)S(1)}, f32[6,128,128]{2,1,0:T(8,128)S(1)}, f32[9,128,128]{2,1,0:T(8,128)S(1)}, f32[9,128,128]{2,1,0:T(8,128)S(1)...) custom-call(s32[6]{0:T(128)S(1)} %copy-done.9, bf16[512,4096]{1,0:T(8,128)(2,1)S(1)} %get-tuple-element.54.refs_1_, ...), custom_call_target="tpu_custom_call" | custom-call | flops 3221225472 | bytes 8388608 | tf_op jit(solution)/shard_map/pair_tiles_0/pallas_call | solution.py:407
  110.9 2.8 %collective-permute-done.11.diag_got = f32[256,512]{1,0:T(8,128)S(1)} collective-permute-done((f32[256,512]{1,0:T(8,128)S(1)}, f32[256,512]{1,0:T(8,128)S(1)}, u32[]{:S(2)}, u32[]{:S(2)}) %collective-permute-start.11) | collective-permute-done | bytes 524320 | tf_op jit(solution)/shard_map/ppermute | solution.py:320
  113.8 3.1 %collective-permute-start.12 = (f32[9,128,128]{2,1,0:T(8,128)S(1)}, f32[9,128,128]{2,1,0:T(8,128)S(1)}, u32[]{:S(2)}, u32[]{:S(2)}) collective-permute-start(f32[9,128,128]{2,1,0:T(8,128)S(1)} %get-tuple-element.71), channel_id=1, source_target_pairs={{0,2},{2,0},{5,7},{7,5},{8,10},{10,8},{13,15},{15,13},{16,18},{18,... | collective-permute-start | bytes 1769480 | tf_op jit(solution)/shard_map/ppermute | solution.py:320
  116.8 0.9 collective-permute-start.13
  117.8 3.6 %pair_tiles_1.1 = (f32[512,256]{1,0:T(8,128)S(1)}, f32[512,256]{1,0:T(8,128)S(1)}, f32[256,512]{1,0:T(8,128)S(1)}, f32[256,256]{1,0:T(8,128)S(1)}) custom-call(s32[6]{0:T(128)S(1)} %copy-done.9, bf16[512,4096]{1,0:T(8,128)(2,1)S(1)} %get-tuple-element.54.refs_1_, bf16[2048,256]{1,0:T(8,128)(2,1)S(1)} %collective-permute-done.9.refs_2_, ...), custom_call_target="tpu_custom_call" | custom-call | flops 1610612736 | bytes 4194304 | tf_op jit(solution)/shard_map/pair_tiles_1/pallas_call | solution.py:407
  121.4 5.8 %collective-permute-done.7.refs_2_ = bf16[2048,256]{1,0:T(8,128)(2,1)S(1)} collective-permute-done((bf16[2048,256]{1,0:T(8,128)(2,1)S(1)}, bf16[2048,256]{1,0:T(8,128)(2,1)S(1)}, u32[]{:S(2)}, u32[]{:S(2)}) %collective-permute-start.7) | collective-permute-done | bytes 1048608 | tf_op jit(solution)/shard_map/ppermute | solution.py:320
  127.2 3.9 %pair_tiles_2.1 = (f32[6,128,128]{2,1,0:T(8,128)S(1)}, bf16[6,128,128]{2,1,0:T(8,128)(2,1)S(1)}, f32[15,128,128]{2,1,0:T(8,128)S(1)}, bf16[15,128,128]{2,1,0:T(8,128)(2,1)S(1)}) custom-call(s32[6]{0:T(128)S(1)} %copy-done.9, bf16[512,4096]{1,0:T(8,128)(2,1)S(1)} %get-tuple-element.54.refs_1_, bf16[2048,256]{1,0:T(8,128)(2,1)S(1)} %collective-permute-done.7.refs_2_, ...), custom_call_target="tpu_custom_call" | custom-call | flops 1610612736 | bytes 4194304 | tf_op jit(solution)/shard_map/pair_tiles_2/pallas_call | solution.py:407
  131.1 1.0 copy-done.2
  132.1 0.7 copy-done.5
  132.8 1.1 collective-permute-done.13.refs_2_
  134.0 3.1 %collective-permute-start.15 = (bf16[15,128,128]{2,1,0:T(8,128)(2,1)S(1)}, bf16[15,128,128]{2,1,0:T(8,128)(2,1)S(1)}, u32[]{:S(2)}, u32[]{:S(2)}) collective-permute-start(bf16[15,128,128]{2,1,0:T(8,128)(2,1)S(1)} %get-tuple-element.81), channel_id=1, source_target_pairs={{0,2},{2,0},{5,7},{7,5},{8,10},{10,8},{13,15},{15,13},{16,18},{18,... | collective-permute-start | bytes 1474568 | tf_op jit(solution)/shard_map/ppermute | solution.py:320
  137.0 0.9 collective-permute-start.14
  138.0 2.9 %strips_0.1 = (f32[2,128,256]{2,1,0:T(8,128)}, f32[2,128,256]{2,1,0:T(8,128)}, f32[128,768]{1,0:T(8,128)}, f32[128,768]{1,0:T(8,128)}) custom-call(s32[6]{0:T(128)} %stack.27.pos_ref.refs_0_, f32[6,128,128]{2,1,0:T(8,128)} %copy-done.6, f32[6,128,128]{2,1,0:T(8,128)} %copy-done.18, f32[9,128,128]{2,1,0:T(8,128)} %copy-done.3, f32[9,128,128]{2,1,0:T(8,128)} %copy-done.15), custom_call_target="tpu_custom_call" | custom-call | tf_op jit(solution)/shard_map/strips_0/pallas_call | solution.py:431
  140.9 7.8 %collective-permute-start.16 = (f32[128,768]{1,0:T(8,128)}, f32[128,768]{1,0:T(8,128)S(1)}, u32[]{:S(2)}, u32[]{:S(2)}) collective-permute-start(f32[128,768]{1,0:T(8,128)} %get-tuple-element.84), channel_id=1, source_target_pairs={{0,5},{2,7},{5,0},{7,2},{8,13},{10,15},{13,8},{15,10},{16,21},{18,... | collective-permute-start | bytes 1179656 | tf_op jit(solution)/shard_map/ppermute | solution.py:320
  148.7 1.9 %collective-permute-start.17 = (f32[128,768]{1,0:T(8,128)}, f32[128,768]{1,0:T(8,128)S(1)}, u32[]{:S(2)}, u32[]{:S(2)}) collective-permute-start(f32[128,768]{1,0:T(8,128)} %get-tuple-element.85), channel_id=1, source_target_pairs={{0,9},{2,11},{4,13},{6,15},{8,17},{9,0},{10,19},{11,2},{12,21},{13... | collective-permute-start | bytes 1179656 | tf_op jit(solution)/shard_map/ppermute | solution.py:320
  150.7 0.6 copy-done.23
  151.5 2.9 %strips_1.1 = (f32[2,128,256]{2,1,0:T(8,128)}, f32[2,128,256]{2,1,0:T(8,128)}, bf16[128,1280]{1,0:T(8,128)(2,1)}, bf16[128,1280]{1,0:T(8,128)(2,1)}) custom-call(s32[6]{0:T(128)} %stack.27.pos_ref.refs_0_, f32[6,128,128]{2,1,0:T(8,128)} %copy-done.5, bf16[6,128,128]{2,1,0:T(8,128)(2,1)} %copy-done.23, f32[15,128,128]{2,1,0:T(8,128)} %copy-done.2, ...), custom_call_target="tpu_custom_call" | custom-call | tf_op jit(solution)/shard_map/strips_1/pallas_call | solution.py:431
  154.5 3.4 %collective-permute-start.18 = (bf16[128,1280]{1,0:T(8,128)(2,1)}, bf16[128,1280]{1,0:T(8,128)(2,1)S(1)}, u32[]{:S(2)}, u32[]{:S(2)}) collective-permute-start(bf16[128,1280]{1,0:T(8,128)(2,1)} %get-tuple-element.86), channel_id=1, source_target_pairs={{0,5},{2,7},{5,0},{7,2},{8,13},{10,15},{13,8},{15,10},{16,21},{18,... | collective-permute-start | bytes 983048 | tf_op jit(solution)/shard_map/ppermute | solution.py:320
  157.9 1.9 %collective-permute-start.19 = (bf16[128,1280]{1,0:T(8,128)(2,1)}, bf16[128,1280]{1,0:T(8,128)(2,1)S(1)}, u32[]{:S(2)}, u32[]{:S(2)}) collective-permute-start(bf16[128,1280]{1,0:T(8,128)(2,1)} %get-tuple-element.87), channel_id=1, source_target_pairs={{0,9},{2,11},{4,13},{6,15},{8,17},{9,0},{10,19},{11,2},{12,21},{13... | collective-permute-start | bytes 983048 | tf_op jit(solution)/shard_map/ppermute | solution.py:320
  159.8 3.2 %collective-permute-done.18.y_1 = bf16[128,1280]{1,0:T(8,128)(2,1)S(1)} collective-permute-done((bf16[128,1280]{1,0:T(8,128)(2,1)}, bf16[128,1280]{1,0:T(8,128)(2,1)S(1)}, u32[]{:S(2)}, u32[]{:S(2)}) %collective-permute-start.18) | collective-permute-done | bytes 327712 | tf_op jit(solution)/shard_map/ppermute | solution.py:320
  163.1 3.4 %collective-permute-done.19.z_1 = bf16[128,1280]{1,0:T(8,128)(2,1)S(1)} collective-permute-done((bf16[128,1280]{1,0:T(8,128)(2,1)}, bf16[128,1280]{1,0:T(8,128)(2,1)S(1)}, u32[]{:S(2)}, u32[]{:S(2)}) %collective-permute-start.19) | collective-permute-done | bytes 327712 | tf_op jit(solution)/shard_map/ppermute | solution.py:320
  166.5 0.7 copy-done.22
  167.2 3.6 %combine.1 = (f32[4,128,512]{2,1,0:T(8,128)}, f32[4,128,512]{2,1,0:T(8,128)}) custom-call(s32[6]{0:T(128)} %stack.27.pos_ref.refs_0_, f32[2,128,256]{2,1,0:T(8,128)} %get-tuple-element.76.held_b0, f32[2,128,256]{2,1,0:T(8,128)} %get-tuple-element.77.held_c0, f32[2,128,256]{2,1,0:T(8,128)} %get-tuple-element.82.held_b1, ...), custom_call_target="tpu_custom_call" | custom-call | tf_op jit(solution)/shard_map/combine/pallas_call | solution.py:442
  170.7 2.9 %collective-permute-done.20.sib = f32[4,128,512]{2,1,0:T(8,128)S(1)} collective-permute-done((f32[4,128,512]{2,1,0:T(8,128)}, f32[4,128,512]{2,1,0:T(8,128)S(1)}, u32[]{:S(2)}, u32[]{:S(2)}) %collective-permute-start.20) | collective-permute-done | bytes 1048608 | tf_op jit(solution)/shard_map/ppermute | solution.py:320
  173.6 1.0 copy-done.14
  174.6 2.6 %finish.1 = (bf16[1,3,128,512]{3,2,1,0:T(8,128)(2,1)}, bf16[1,2,128,512]{3,2,1,0:T(8,128)(2,1)}) custom-call(s32[6]{0:T(128)} %stack.27.pos_ref.refs_0_, s32[1,3]{1,0:T(1,128)} %offsets_ref.3, f32[4,128,512]{2,1,0:T(8,128)} %get-tuple-element.90.mine, f32[4,128,512]{2,1,0:T(8,128)} %copy-done.14), custom_call_target="tpu_custom_call" | custom-call | tf_op jit(solution)/shard_map/finish/pallas_call | solution.py:450
  (60 shorter events, 1.5 us)
Async XLA Ops:
  0.6 67.3 %copy-start = (bf16[4096,512]{1,0:T(8,128)(2,1)S(1)}, bf16[4096,512]{1,0:T(8,128)(2,1)}, u32[]{:S(2)}) copy-start(bf16[4096,512]{1,0:T(8,128)(2,1)} %x_ref.2) | copy-start | bytes 12582916
  65.3 36.6 %collective-permute-start.5 = (bf16[4096,256]{1,0:T(8,128)(2,1)}, bf16[4096,256]{1,0:T(8,128)(2,1)}, u32[]{:S(2)}, u32[]{:S(2)}) collective-permute-start(bf16[4096,256]{1,0:T(8,128)(2,1)} %first_chunk.1), channel_id=1, source_target_pairs={{1,5},{3,7},{4,0},{6,2},{9,13},{11,15},{12,8},{14,10},{17,21},{19,... | collective-permute-start | bytes 6291464 | tf_op jit(solution)/shard_map/ppermute | solution.py:320
  66.6 36.6 %collective-permute-start.6 = (bf16[4096,256]{1,0:T(8,128)(2,1)}, bf16[4096,256]{1,0:T(8,128)(2,1)}, u32[]{:S(2)}, u32[]{:S(2)}) collective-permute-start(bf16[4096,256]{1,0:T(8,128)(2,1)} %first_chunk.1), channel_id=1, source_target_pairs={{1,9},{3,11},{5,13},{7,15},{8,0},{9,17},{10,2},{11,19},{12,4},{13,... | collective-permute-start | bytes 6291464 | tf_op jit(solution)/shard_map/ppermute | solution.py:320
  70.2 1.0 copy-start.11
  71.2 12.2 %copy-start.10 = (f32[2,512]{1,0:T(2,128)}, f32[2,512]{1,0:T(2,128)S(1)}, u32[]{:S(2)}) copy-start(f32[2,512]{1,0:T(2,128)S(1)} %get-tuple-element.48.own_ref) | copy-start | bytes 12292
  71.2 10.5 %collective-permute-start = (f32[2,512]{1,0:T(2,128)S(1)}, f32[2,512]{1,0:T(2,128)S(1)}, u32[]{:S(2)}, u32[]{:S(2)}) collective-permute-start(f32[2,512]{1,0:T(2,128)S(1)} %get-tuple-element.48.own_ref), channel_id=1, source_target_pairs={{0,1},{1,0},{2,3},{3,2},{4,5},{5,4},{6,7},{7,6},{8,9},{9,8},{10,11... | collective-permute-start | bytes 12296 | tf_op jit(solution)/shard_map/ppermute | solution.py:320
  78.9 3.6 %collective-permute-start.1 = (f32[2,512]{1,0:T(2,128)S(1)}, f32[2,512]{1,0:T(2,128)S(1)}, u32[]{:S(2)}, u32[]{:S(2)}) collective-permute-start(f32[2,512]{1,0:T(2,128)S(1)} %get-tuple-element.48.own_ref), channel_id=1, source_target_pairs={{0,2},{1,3},{2,0},{3,1},{4,6},{5,7},{6,4},{7,5},{8,10},{9,11},{10,... | collective-permute-start | bytes 12296 | tf_op jit(solution)/shard_map/ppermute | solution.py:320
  80.4 3.0 %collective-permute-start.2 = (f32[2,512]{1,0:T(2,128)S(1)}, f32[2,512]{1,0:T(2,128)S(1)}, u32[]{:S(2)}, u32[]{:S(2)}) collective-permute-start(f32[2,512]{1,0:T(2,128)S(1)} %get-tuple-element.48.own_ref), channel_id=1, source_target_pairs={{0,3},{1,2},{2,1},{3,0},{4,7},{5,6},{6,5},{7,4},{8,11},{9,10},{10,... | collective-permute-start | bytes 12296 | tf_op jit(solution)/shard_map/ppermute | solution.py:320
  81.6 1.8 %copy-start.24 = (f32[2,512]{1,0:T(2,128)}, f32[2,512]{1,0:T(2,128)S(1)}, u32[]{:S(2)}) copy-start(f32[2,512]{1,0:T(2,128)S(1)} %collective-permute-done.sib_ref) | copy-start | bytes 12292
  82.5 0.9 copy-start.25
  83.4 0.6 copy-start.26
  85.5 12.5 %collective-permute-start.3 = (f32[4,512]{1,0:T(4,128)}, f32[4,512]{1,0:T(4,128)S(1)}, u32[]{:S(2)}, u32[]{:S(2)}) collective-permute-start(f32[4,512]{1,0:T(4,128)} %get-tuple-element.51.refs_4_), channel_id=1, source_target_pairs={{0,9},{2,11},{4,13},{6,15},{8,17},{9,0},{10,19},{11,2},{12,21},{13... | collective-permute-start | bytes 24584 | tf_op jit(solution)/shard_map/ppermute | solution.py:320
  87.4 10.6 %collective-permute-start.4 = (f32[4,512]{1,0:T(4,128)}, f32[4,512]{1,0:T(4,128)S(1)}, u32[]{:S(2)}, u32[]{:S(2)}) collective-permute-start(f32[4,512]{1,0:T(4,128)} %get-tuple-element.51.refs_4_), channel_id=1, source_target_pairs={{0,5},{2,7},{5,0},{7,2},{8,13},{10,15},{13,8},{15,10},{16,21},{18,... | collective-permute-start | bytes 24584 | tf_op jit(solution)/shard_map/ppermute | solution.py:320
  89.3 2.2 %copy-start.1 = (bf16[4096,512]{1,0:T(8,128)(2,1)S(1)}, bf16[4096,512]{1,0:T(8,128)(2,1)}, u32[]{:S(2)}) copy-start(bf16[4096,512]{1,0:T(8,128)(2,1)} %x_ref.2) | copy-start | bytes 12582916
  91.5 0.6 copy-start.8
  92.1 0.7 copy-start.13
  92.8 5.2 %copy-start.12 = (bf16[2048,256]{1,0:T(8,128)(2,1)S(1)}, bf16[2048,256]{1,0:T(8,128)(2,1)}, u32[]{:S(2)}) copy-start(bf16[2048,256]{1,0:T(8,128)(2,1)} %copy-done.11) | copy-start | bytes 3145732
  92.8 11.6 %copy-start.7 = (f32[4,512]{1,0:T(4,128)S(1)}, f32[4,512]{1,0:T(4,128)}, u32[]{:S(2)}) copy-start(f32[4,512]{1,0:T(4,128)} %get-tuple-element.51.refs_4_) | copy-start | bytes 24580
  92.8 11.6 %copy-start.9 = (s32[6]{0:T(128)S(1)}, s32[6]{0:T(128)}, u32[]{:S(2)}) copy-start(s32[6]{0:T(128)} %stack.27.pos_ref.refs_0_) | copy-start | bytes 76
  97.1 0.8 copy-start.4
  97.9 18.9 %collective-permute-start.10 = (bf16[2048,256]{1,0:T(8,128)(2,1)S(1)}, bf16[2048,256]{1,0:T(8,128)(2,1)S(1)}, u32[]{:S(2)}, u32[]{:S(2)}) collective-permute-start(bf16[2048,256]{1,0:T(8,128)(2,1)S(1)} %copy-done.12), channel_id=1, source_target_pairs={{1,9},{3,11},{5,13},{7,15},{8,0},{9,17},{10,2},{11,19},{12,4},{13,... | collective-permute-start | bytes 3145736 | tf_op jit(solution)/shard_map/ppermute | solution.py:320
  99.2 18.5 %collective-permute-start.9 = (bf16[2048,256]{1,0:T(8,128)(2,1)S(1)}, bf16[2048,256]{1,0:T(8,128)(2,1)S(1)}, u32[]{:S(2)}, u32[]{:S(2)}) collective-permute-start(bf16[2048,256]{1,0:T(8,128)(2,1)S(1)} %copy-done.12), channel_id=1, source_target_pairs={{1,5},{3,7},{4,0},{6,2},{9,13},{11,15},{12,8},{14,10},{17,21},{19,... | collective-permute-start | bytes 3145736 | tf_op jit(solution)/shard_map/ppermute | solution.py:320
  100.5 26.6 %collective-permute-start.7 = (bf16[2048,256]{1,0:T(8,128)(2,1)S(1)}, bf16[2048,256]{1,0:T(8,128)(2,1)S(1)}, u32[]{:S(2)}, u32[]{:S(2)}) collective-permute-start(bf16[2048,256]{1,0:T(8,128)(2,1)S(1)} %get-tuple-element.58), channel_id=1, source_target_pairs={{1,5},{3,7},{4,0},{6,2},{9,13},{11,15},{12,8},{14,10},{17,21},{19,... | collective-permute-start | bytes 3145736 | tf_op jit(solution)/shard_map/ppermute | solution.py:320
  101.9 25.3 %collective-permute-start.8 = (bf16[2048,256]{1,0:T(8,128)(2,1)S(1)}, bf16[2048,256]{1,0:T(8,128)(2,1)S(1)}, u32[]{:S(2)}, u32[]{:S(2)}) collective-permute-start(bf16[2048,256]{1,0:T(8,128)(2,1)S(1)} %get-tuple-element.58), channel_id=1, source_target_pairs={{1,9},{3,11},{5,13},{7,15},{8,0},{9,17},{10,2},{11,19},{12,4},{13,... | collective-permute-start | bytes 3145736 | tf_op jit(solution)/shard_map/ppermute | solution.py:320
  103.2 10.6 %collective-permute-start.11 = (f32[256,512]{1,0:T(8,128)S(1)}, f32[256,512]{1,0:T(8,128)S(1)}, u32[]{:S(2)}, u32[]{:S(2)}) collective-permute-start(f32[256,512]{1,0:T(8,128)S(1)} %get-tuple-element.70), channel_id=1, source_target_pairs={{0,2},{1,3},{2,0},{3,1},{4,6},{5,7},{6,4},{7,5},{8,10},{9,11},{10,... | collective-permute-start | bytes 1572872 | tf_op jit(solution)/shard_map/ppermute | solution.py:320
  110.9 10.5 %copy-start.3 = (f32[9,128,128]{2,1,0:T(8,128)}, f32[9,128,128]{2,1,0:T(8,128)S(1)}, u32[]{:S(2)}) copy-start(f32[9,128,128]{2,1,0:T(8,128)S(1)} %get-tuple-element.74.refs_3_) | copy-start | bytes 1769476
  110.9 10.5 %copy-start.6 = (f32[6,128,128]{2,1,0:T(8,128)}, f32[6,128,128]{2,1,0:T(8,128)S(1)}, u32[]{:S(2)}) copy-start(f32[6,128,128]{2,1,0:T(8,128)S(1)} %get-tuple-element.57.refs_1_) | copy-start | bytes 1179652
  113.8 4.0 %copy-start.16 = (f32[256,512]{1,0:T(8,128)}, f32[256,512]{1,0:T(8,128)S(1)}, u32[]{:S(2)}) copy-start(f32[256,512]{1,0:T(8,128)S(1)} %collective-permute-done.11.diag_got) | copy-start | bytes 1572868
  113.8 20.2 %collective-permute-start.12 = (f32[9,128,128]{2,1,0:T(8,128)S(1)}, f32[9,128,128]{2,1,0:T(8,128)S(1)}, u32[]{:S(2)}, u32[]{:S(2)}) collective-permute-start(f32[9,128,128]{2,1,0:T(8,128)S(1)} %get-tuple-element.71), channel_id=1, source_target_pairs={{0,2},{2,0},{5,7},{7,5},{8,10},{10,8},{13,15},{15,13},{16,18},{18,... | collective-permute-start | bytes 1769480 | tf_op jit(solution)/shard_map/ppermute | solution.py:320
  116.8 17.1 %collective-permute-start.13 = (f32[6,128,128]{2,1,0:T(8,128)S(1)}, f32[6,128,128]{2,1,0:T(8,128)S(1)}, u32[]{:S(2)}, u32[]{:S(2)}) collective-permute-start(f32[6,128,128]{2,1,0:T(8,128)S(1)} %get-tuple-element.72), channel_id=1, source_target_pairs={{0,2},{1,3},{2,0},{3,1},{4,6},{5,7},{6,4},{7,5},{8,10},{9,11},{10,... | collective-permute-start | bytes 1179656 | tf_op jit(solution)/shard_map/ppermute | solution.py:320
  131.1 1.0 copy-start.2
  132.1 0.7 copy-start.5
  134.0 4.0 %copy-start.18 = (f32[6,128,128]{2,1,0:T(8,128)}, f32[6,128,128]{2,1,0:T(8,128)S(1)}, u32[]{:S(2)}) copy-start(f32[6,128,128]{2,1,0:T(8,128)S(1)} %collective-permute-done.13.refs_2_) | copy-start | bytes 1179652
  134.0 4.0 %copy-start.15 = (f32[9,128,128]{2,1,0:T(8,128)}, f32[9,128,128]{2,1,0:T(8,128)S(1)}, u32[]{:S(2)}) copy-start(f32[9,128,128]{2,1,0:T(8,128)S(1)} %collective-permute-done.12.refs_4_) | copy-start | bytes 1769476
  134.0 16.7 %collective-permute-start.15 = (bf16[15,128,128]{2,1,0:T(8,128)(2,1)S(1)}, bf16[15,128,128]{2,1,0:T(8,128)(2,1)S(1)}, u32[]{:S(2)}, u32[]{:S(2)}) collective-permute-start(bf16[15,128,128]{2,1,0:T(8,128)(2,1)S(1)} %get-tuple-element.81), channel_id=1, source_target_pairs={{0,2},{2,0},{5,7},{7,5},{8,10},{10,8},{13,15},{15,13},{16,18},{18,... | collective-permute-start | bytes 1474568 | tf_op jit(solution)/shard_map/ppermute | solution.py:320
  137.0 13.6 %collective-permute-start.14 = (bf16[6,128,128]{2,1,0:T(8,128)(2,1)S(1)}, bf16[6,128,128]{2,1,0:T(8,128)(2,1)S(1)}, u32[]{:S(2)}, u32[]{:S(2)}) collective-permute-start(bf16[6,128,128]{2,1,0:T(8,128)(2,1)S(1)} %get-tuple-element.79), channel_id=1, source_target_pairs={{0,2},{1,3},{2,0},{3,1},{4,6},{5,7},{6,4},{7,5},{8,10},{9,11},{10,... | collective-permute-start | bytes 589832 | tf_op jit(solution)/shard_map/ppermute | solution.py:320
  140.9 18.9 %collective-permute-start.16 = (f32[128,768]{1,0:T(8,128)}, f32[128,768]{1,0:T(8,128)S(1)}, u32[]{:S(2)}, u32[]{:S(2)}) collective-permute-start(f32[128,768]{1,0:T(8,128)} %get-tuple-element.84), channel_id=1, source_target_pairs={{0,5},{2,7},{5,0},{7,2},{8,13},{10,15},{13,8},{15,10},{16,21},{18,... | collective-permute-start | bytes 1179656 | tf_op jit(solution)/shard_map/ppermute | solution.py:320
  148.7 11.1 %collective-permute-start.17 = (f32[128,768]{1,0:T(8,128)}, f32[128,768]{1,0:T(8,128)S(1)}, u32[]{:S(2)}, u32[]{:S(2)}) collective-permute-start(f32[128,768]{1,0:T(8,128)} %get-tuple-element.85), channel_id=1, source_target_pairs={{0,9},{2,11},{4,13},{6,15},{8,17},{9,0},{10,19},{11,2},{12,21},{13... | collective-permute-start | bytes 1179656 | tf_op jit(solution)/shard_map/ppermute | solution.py:320
  150.6 0.7 copy-start.23
  150.7 0.8 copy-start.17
  154.5 8.6 %collective-permute-start.18 = (bf16[128,1280]{1,0:T(8,128)(2,1)}, bf16[128,1280]{1,0:T(8,128)(2,1)S(1)}, u32[]{:S(2)}, u32[]{:S(2)}) collective-permute-start(bf16[128,1280]{1,0:T(8,128)(2,1)} %get-tuple-element.86), channel_id=1, source_target_pairs={{0,5},{2,7},{5,0},{7,2},{8,13},{10,15},{13,8},{15,10},{16,21},{18,... | collective-permute-start | bytes 983048 | tf_op jit(solution)/shard_map/ppermute | solution.py:320
  157.9 8.6 %collective-permute-start.19 = (bf16[128,1280]{1,0:T(8,128)(2,1)}, bf16[128,1280]{1,0:T(8,128)(2,1)S(1)}, u32[]{:S(2)}, u32[]{:S(2)}) collective-permute-start(bf16[128,1280]{1,0:T(8,128)(2,1)} %get-tuple-element.87), channel_id=1, source_target_pairs={{0,9},{2,11},{4,13},{6,15},{8,17},{9,0},{10,19},{11,2},{12,21},{13... | collective-permute-start | bytes 983048 | tf_op jit(solution)/shard_map/ppermute | solution.py:320
  159.8 6.7 %copy-start.19 = (f32[128,768]{1,0:T(8,128)}, f32[128,768]{1,0:T(8,128)S(1)}, u32[]{:S(2)}) copy-start(f32[128,768]{1,0:T(8,128)S(1)} %collective-permute-done.16.y_0) | copy-start | bytes 1179652
  159.8 6.7 %copy-start.20 = (f32[128,768]{1,0:T(8,128)}, f32[128,768]{1,0:T(8,128)S(1)}, u32[]{:S(2)}) copy-start(f32[128,768]{1,0:T(8,128)S(1)} %collective-permute-done.17.z_0) | copy-start | bytes 1179652
  163.1 3.4 %copy-start.21 = (bf16[128,1280]{1,0:T(8,128)(2,1)}, bf16[128,1280]{1,0:T(8,128)(2,1)S(1)}, u32[]{:S(2)}) copy-start(bf16[128,1280]{1,0:T(8,128)(2,1)S(1)} %collective-permute-done.18.y_1) | copy-start | bytes 983044
  166.5 0.7 copy-start.22
  170.7 2.9 %collective-permute-start.20 = (f32[4,128,512]{2,1,0:T(8,128)}, f32[4,128,512]{2,1,0:T(8,128)S(1)}, u32[]{:S(2)}, u32[]{:S(2)}) collective-permute-start(f32[4,128,512]{2,1,0:T(8,128)} %get-tuple-element.91), channel_id=1, source_target_pairs={{0,1},{1,0},{2,3},{3,2},{4,5},{5,4},{6,7},{7,6},{8,9},{9,8},{10,11... | collective-permute-start | bytes 3145736 | tf_op jit(solution)/shard_map/ppermute | solution.py:320
  173.6 1.0 copy-start.14

commit v2 on v0

--- a/solution.py
+++ b/solution.py
@@ -11,7 +11,8 @@
 BF16 = jnp.bfloat16
 VMEM = pl.BlockSpec(memory_space=pltpu.VMEM)
 SMEM = pl.BlockSpec(memory_space=pltpu.SMEM)
-BIG = pltpu.CompilerParams(vmem_limit_bytes=56 << 20)
+SOME = pltpu.CompilerParams(vmem_limit_bytes=24 << 20)
+MOST = pltpu.CompilerParams(vmem_limit_bytes=58 << 20)
 D_BLOCKS = {0: [(0, 0)], 1: [(0, 1), (1, 0), (1, 1)]}
 
 
@@ -23,15 +24,21 @@
     return ((raw.astype(F32) - stat_ref[0:1, :]) * stat_ref[1:2, :]).astype(BF16)
 
 
-def first_kernel(steps, x_ref, chunk_0, chunk_1, out_ref, center, total, square):
+def cut_kernel(left_ref, right_ref, out_ref):
+    strip = left_ref.shape[1]
+    out_ref[:, :strip] = left_ref[...]
+    out_ref[:, strip:] = right_ref[...]
+
+
+def first_kernel(steps, x_ref, copy_ref, chunk_ref, out_ref, center, total, square):
     step = pl.program_id(0)
     rows, width = x_ref.shape
-    strip = chunk_0.shape[1] // 2
+    strip = chunk_ref.shape[1] // 2
     group = min(64, rows)
-    for part, out in enumerate((chunk_0, chunk_1)):
-        for half in range(2):
-            start = (2 * half + part) * strip
-            out[:, half * strip:(half + 1) * strip] = x_ref[:, start:start + strip]
+    copy_ref[...] = x_ref[...]
+    for half in range(2):
+        start = (2 * half + 1) * strip
+        chunk_ref[:, half * strip:(half + 1) * strip] = x_ref[:, start:start + strip]
 
     @pl.when(step == 0)
     def _():
@@ -121,9 +128,10 @@
 def pair_kernel(chunk, *refs):
     (pos_ref, turned_ref, y_ref, w_ref, stat_ref, ystat_ref, wstat_ref), refs = refs[:7], refs[7:]
     if chunk == 0:
-        keep_c, send_c, keep_bd, send_bd, yt_out, w_out, acc_b, acc_c, acc_d = refs
+        (keep_c, send_c, keep_bd, send_bd, yt_out, w_out), accs = refs[:6], refs[6:]
     else:
-        yt_old, w_old, keep_c, send_c, keep_bd, send_bd, acc_b, acc_c, acc_d, acc_e = refs
+        (yt_old, w_old, keep_c, send_c, keep_bd, send_bd), accs = refs[:6], refs[6:]
+    acc_b, acc_c, acc_d = accs[:3]
     step = pl.program_id(0)
     last = pl.num_programs(0) - 1
     x = pos_ref[0]
@@ -132,7 +140,7 @@
 
     @pl.when(step == 0)
     def _():
-        for acc in (acc_b, acc_c, acc_d) + (() if chunk == 0 else (acc_e,)):
+        for acc in accs:
             acc[...] = jnp.zeros_like(acc)
 
     zt = turned_ref[...]
@@ -150,7 +158,7 @@
             yt_out[...] = yt
             acc_d[...] += dot(yt, w)
         else:
-            acc_e[...] += dot(yt_old[...], w)
+            accs[3][...] += dot(yt_old[...], w)
             acc_d[:, :2 * size] += dot(yt, w_old[...])
             acc_d[:, 2 * size:] += dot(yt, w)
 
@@ -170,6 +178,7 @@
             if chunk == 0:
                 put_blocks(x, acc_d, 0, keep_bd, send_bd, 6, 1)
             else:
+                acc_e = accs[3]
                 acc_d[:, 2 * size:] *= scale
                 acc_e[...] *= scale
                 put_blocks(x, acc_e, 0, keep_bd, send_bd, 6, 1)
@@ -307,29 +316,39 @@
     flat = lambda rows: pl.BlockSpec((rows, step_rows), lambda k: (0, k))
     whole = lambda *shape: pl.BlockSpec(shape, lambda k: (0,) * len(shape))
 
-    chunk_0, chunk_1, local = pl.pallas_call(
+    chunk_0 = pl.pallas_call(
+        cut_kernel,
+        grid=(steps,),
+        in_specs=[pl.BlockSpec((step_rows, strip), lambda k, half=half: (k, 2 * half)) for half in range(2)],
+        out_specs=tall,
+        out_shape=jax.ShapeDtypeStruct((depth, half), BF16),
+        compiler_params=MOST,
+        cost_estimate=pl.CostEstimate(flops=0, bytes_accessed=2 * depth * width, transcendentals=0),
+        name="first_chunk",
+    )(dosage, dosage)
+    w_raw, y_raw = [send(chunk_0, z_main)], [send(chunk_0, y_main)]
+    dosage, chunk_0 = lax.optimization_barrier((dosage, chunk_0))
+    block, chunk_1, local = pl.pallas_call(
         lambda *refs: first_kernel(steps, *refs),
         grid=(steps,),
         in_specs=[wide],
-        out_specs=[tall, tall, whole(2, width)],
-        out_shape=[jax.ShapeDtypeStruct((depth, half), BF16)] * 2 + [jax.ShapeDtypeStruct((2, width), F32)],
+        out_specs=[wide, tall, whole(2, width)],
+        out_shape=[jax.ShapeDtypeStruct((depth, width), BF16), jax.ShapeDtypeStruct((depth, half), BF16),
+                   jax.ShapeDtypeStruct((2, width), F32)],
         scratch_shapes=[pltpu.VMEM((1, width), F32)] + [pltpu.VMEM((8, width), F32)] * 2,
-        compiler_params=BIG,
-        cost_estimate=pl.CostEstimate(flops=5 * depth * width, bytes_accessed=4 * depth * width, transcendentals=0),
-        name="chunks_and_local_stats",
+        compiler_params=SOME,
+        cost_estimate=pl.CostEstimate(flops=5 * depth * width, bytes_accessed=5 * depth * width, transcendentals=0),
+        name="second_chunk_and_local_stats",
     )(dosage)
-    w_raw, y_raw = [send(chunk_0, z_main)], [send(chunk_0, y_main)]
     others = [send(local, [(at(a, b), at(a, b ^ flip)) for a, b in everyone]) for flip in (1, 2, 3)]
     stat, stat_chunked = pl.pallas_call(
         stat_kernel,
         in_specs=[SMEM, SMEM, SMEM] + [VMEM] * 4,
         out_specs=[VMEM, VMEM],
         out_shape=[jax.ShapeDtypeStruct((4, width), F32)] * 2,
+        compiler_params=SOME,
         name="stats",
     )(pos, live_counts, pair_offsets, local, *others)
-    stat, chunk_1 = lax.optimization_barrier((stat, chunk_1))
-    w_raw.append(send(chunk_1, z_main))
-    y_raw.append(send(chunk_1, y_main))
     z_step = [(a, b, a + 2 if b % 2 == 0 else a - 2) for a, b in everyone]
     z_cross = [(at(a, b), at(t, b ^ 1)) for a, b, t in z_step if 0 <= t < n_var]
     y_cross = [(at(a, b), at(a ^ 1, b ^ 1)) for a, b in everyone if active_on(a, b)]
@@ -342,34 +361,35 @@
         out_specs=[flat(width)] + [whole(half, width)] * 2,
         out_shape=[jax.ShapeDtypeStruct((width, depth), BF16)] + [jax.ShapeDtypeStruct((half, width), F32)] * 2,
         scratch_shapes=[pltpu.VMEM((width, width), F32)],
-        compiler_params=BIG,
+        compiler_params=SOME,
         cost_estimate=pl.CostEstimate(flops=2 * depth * width * width, bytes_accessed=4 * depth * width, transcendentals=0),
         name="own_tile",
-    )(pos, dosage, stat)
+    )(pos, block, stat)
+    turned, w_stat, y_stat, chunk_1 = lax.optimization_barrier((turned, w_stat, y_stat, chunk_1))
+    w_raw.append(send(chunk_1, z_main))
+    y_raw.append(send(chunk_1, y_main))
     diag_across = send(diag_send, across)
     keeps, arrived, passed, before = [], [], [], [diag_across]
     sent_as = (F32, BF16)
     for part in range(2):
         n_bd = 6 + 3 * len(D_BLOCKS[part])
         in_specs = [SMEM, flat(width), tall, tall] + [pl.BlockSpec((4, half), lambda k, part=part: (0, part))] * 3
-        out_specs = [whole(6, strip, strip)] * 2 + [whole(n_bd, strip, strip)] * 2
+        sums = [(width, half), (width, half), (half, half if part == 0 else width)] + [(half, half)] * part
+        out_specs = [whole(n, strip, strip) for n in (6, 6, n_bd, n_bd)]
         out_shape = [jax.ShapeDtypeStruct((n, strip, strip), kind) for n in (6, n_bd) for kind in (F32, sent_as[part])]
-        scratch = [pltpu.VMEM((width, half), F32)] * 2
         if part == 0:
             out_specs += [flat(half), tall]
             out_shape += [jax.ShapeDtypeStruct((half, depth), BF16), jax.ShapeDtypeStruct((depth, half), BF16)]
-            scratch += [pltpu.VMEM((half, half), F32)]
         else:
             in_specs += [flat(half), tall]
-            scratch += [pltpu.VMEM((half, width), F32), pltpu.VMEM((half, half), F32)]
         keep_c, send_c, keep_bd, send_bd, *passed = pl.pallas_call(
             lambda *refs, part=part: pair_kernel(part, *refs),
             grid=(steps,),
             in_specs=in_specs,
             out_specs=out_specs,
             out_shape=out_shape,
-            scratch_shapes=scratch,
-            compiler_params=BIG,
+            scratch_shapes=[pltpu.VMEM(shape, F32) for shape in sums],
+            compiler_params=SOME,
             cost_estimate=pl.CostEstimate(flops=3 * depth * width * width, bytes_accessed=4 * depth * width, transcendentals=0),
             name=f"pair_tiles_{part}",
         )(pos, turned, y_raw[part], w_raw[part], stat_chunked, y_stat, w_stat, *passed)
@@ -387,6 +407,7 @@
             in_specs=[SMEM] + [VMEM] * 4,
             out_specs=[VMEM] * 4,
             out_shape=[jax.ShapeDtypeStruct((2, strip, half), F32)] * 2 + [sent] * 2,
+            compiler_params=SOME,
             name=f"strips_{part}",
         )(pos, keep_c, arrived[2 + 2 * part], keep_bd, arrived[1 + 2 * part])
         held += [held_b, held_c]
@@ -398,6 +419,7 @@
         in_specs=[SMEM] + [VMEM] * 10,
         out_specs=[VMEM] * 2,
         out_shape=[four] * 2,
+        compiler_params=SOME,
         name="combine",
     )(pos, *held, *sides, diag_keep, arrived[0])
 
@@ -407,6 +429,7 @@
         out_specs=[VMEM, VMEM],
         out_shape=[jax.ShapeDtypeStruct((1, SLOTS, strip, width), BF16),
                    jax.ShapeDtypeStruct((1, 2, strip, width), BF16)],
+        compiler_params=SOME,
         name="finish",
     )(pos, pair_offsets, mine, send(sib, sibling))
 

time: 111 us -> 104 us (0.937)
  Pallas kernels: 45.4 us -> 29.2 us
  waiting for transfers between devices: 20.8 us -> 30.1 us
    ppermute x19, waiting for transfers between devices: 20.8 us -> 30.1 us  [send(): return lax.ppermute(value, AXES, pairs)]
    pallas_call x2, Pallas kernels: 19.1 us -> 13.5 us  [body(): pl.pallas_call(lambda *refs, part=part: pair_kernel(part, *refs), grid=(s...]
    pallas_call x0 -> x1, Pallas kernels: none -> 4.06 us  [body(): pl.pallas_call(cut_kernel, grid=(steps,), in_specs=[pl.BlockSpec((step_ro...]
    pallas_call x2, Pallas kernels: 5.79 us -> 1.76 us  [body(): pl.pallas_call(lambda *refs, part=part: strips_kernel(part, *refs), in_sp...]
    pallas_call x1, Pallas kernels: 5.92 us -> 2.52 us  [body(): pl.pallas_call(lambda *refs: first_kernel(steps, *refs), grid=(steps,), i...]
    pallas_call x1, Pallas kernels: 3.56 us -> 0.79 us  [body(): pl.pallas_call(combine_kernel, in_specs=[SMEM] + [VMEM] * 10, out_specs=[...]
    pallas_call x1, Pallas kernels: 6.92 us -> 4.31 us  [body(): pl.pallas_call(own_kernel, grid=(steps,), in_specs=[SMEM, wide, whole(4,...]
    unnamed x36 -> x12, local copies, waits for them, and re-layouts: 5.86 us -> 5.51 us
  transfers between devices with their start and end apart: 19 -> 19, of which waited for: 9 -> 8; matrix products, arithmetic and copies ran while one was open for 1% -> 0% of each run, Pallas kernels for 30% -> 22%
where the time goes in v2:
time: 104 us; the launch traced here: 103 us
  starting transfers between devices  36.3 us (35%)
  waiting for transfers between devices  30.1 us (29%)
  Pallas kernels  29.2 us (28%)
  local copies, waits for them, and re-layouts  5.6 us (5%)
  between operations  1.53 us (1%)
    ppermute x19, starting transfers between devices, send(): return lax.ppermute(value, AXES, pairs)  36.3 us
    ppermute x19, waiting for transfers between devices, send(): return lax.ppermute(value, AXES, pairs)  30.1 us
    pallas_call x2, Pallas kernels, body(): pl.pallas_call(lambda *refs, part=part: pair_kernel(part, *refs), grid=(s...  13.5 us
    unnamed x12, local copies, waits for them, and re-layouts  5.51 us
    pallas_call x1, Pallas kernels, body(): pl.pallas_call(own_kernel, grid=(steps,), in_specs=[SMEM, wide, whole(4,...  4.31 us
    pallas_call x1, Pallas kernels, body(): pl.pallas_call(cut_kernel, grid=(steps,), in_specs=[pl.BlockSpec((step_ro...  4.06 us
    pallas_call x1, Pallas kernels, body(): pl.pallas_call(lambda *refs: first_kernel(steps, *refs), grid=(steps,), i...  2.52 us
  transfers between devices with their start and end apart: 19, of which 8 were waited for; matrix products, arithmetic and copies ran while one was open for 0% of the time, Pallas kernels for 22%

profile of v2, /device:TPU:0, one launch (start us, length us, event | category | flops | bytes accessed | tf_op | source)
XLA Modules:
  0.0 102.6 jit_solution(15907141714398359191)
XLA Ops:
  0.6 4.1 %first_chunk.1 = bf16[4096,256]{1,0:T(8,128)(2,1)} custom-call(bf16[4096,512]{1,0:T(8,128)(2,1)} %refs_0_, bf16[4096,512]{1,0:T(8,128)(2,1)} %refs_0_), custom_call_target="tpu_custom_call" | custom-call | bytes 4194304 | tf_op jit(solution)/shard_map/first_chunk/pallas_call | solution.py:319
  4.7 1.4 %collective-permute-start.6 = (bf16[4096,256]{1,0:T(8,128)(2,1)}, bf16[4096,256]{1,0:T(8,128)(2,1)}, u32[]{:S(2)}, u32[]{:S(2)}) collective-permute-start(bf16[4096,256]{1,0:T(8,128)(2,1)} %first_chunk.1), channel_id=1, source_target_pairs={{1,9},{3,11},{5,13},{7,15},{8,0},{9,17},{10,2},{11,19},{12,4},{13,... | collective-permute-start | bytes 6291464 | tf_op jit(solution)/shard_map/ppermute | solution.py:309
  6.1 1.3 %collective-permute-start.5 = (bf16[4096,256]{1,0:T(8,128)(2,1)}, bf16[4096,256]{1,0:T(8,128)(2,1)}, u32[]{:S(2)}, u32[]{:S(2)}) collective-permute-start(bf16[4096,256]{1,0:T(8,128)(2,1)} %first_chunk.1), channel_id=1, source_target_pairs={{1,5},{3,7},{4,0},{6,2},{9,13},{11,15},{12,8},{14,10},{17,21},{19,... | collective-permute-start | bytes 6291464 | tf_op jit(solution)/shard_map/ppermute | solution.py:309
  7.4 2.5 %second_chunk_and_local_stats.1 = (bf16[4096,512]{1,0:T(8,128)(2,1)S(1)}, bf16[4096,256]{1,0:T(8,128)(2,1)S(1)}, f32[2,512]{1,0:T(2,128)S(1)}) custom-call(bf16[4096,512]{1,0:T(8,128)(2,1)S(1)} %copy-done), custom_call_target="tpu_custom_call" | custom-call | flops 10485760 | bytes 10485760 | tf_op jit(solution)/shard_map/second_chunk_and_local_stats/pallas_call | solution.py:331
  10.0 2.0 %copy-done.2 = bf16[4096,512]{1,0:T(8,128)(2,1)} copy-done((bf16[4096,512]{1,0:T(8,128)(2,1)}, bf16[4096,512]{1,0:T(8,128)(2,1)S(1)}, u32[]{:S(2)}) %copy-start.2) | copy-done | bytes 4194328
  11.9 1.4 %copy-done.4 = bf16[4096,256]{1,0:T(8,128)(2,1)} copy-done((bf16[4096,256]{1,0:T(8,128)(2,1)}, bf16[4096,256]{1,0:T(8,128)(2,1)S(1)}, u32[]{:S(2)}) %copy-start.4) | copy-done | bytes 2097176
  13.3 8.9 %collective-permute-start.2 = (f32[2,512]{1,0:T(2,128)S(1)}, f32[2,512]{1,0:T(2,128)S(1)}, u32[]{:S(2)}, u32[]{:S(2)}) collective-permute-start(f32[2,512]{1,0:T(2,128)S(1)} %get-tuple-element.44.own_ref), channel_id=1, source_target_pairs={{0,3},{1,2},{2,1},{3,0},{4,7},{5,6},{6,5},{7,4},{8,11},{9,10},{10,... | collective-permute-start | bytes 12296 | tf_op jit(solution)/shard_map/ppermute | solution.py:309
  22.1 0.5 collective-permute-start.1
  22.7 0.0 collective-permute-start
  23.3 0.1 stack.27.pos_ref.refs_0_
  23.4 0.1 collective-permute-done.2.cross_ref
  23.5 2.3 %collective-permute-done.1.far_ref = f32[2,512]{1,0:T(2,128)S(1)} collective-permute-done((f32[2,512]{1,0:T(2,128)S(1)}, f32[2,512]{1,0:T(2,128)S(1)}, u32[]{:S(2)}, u32[]{:S(2)}) %collective-permute-start.1) | collective-permute-done | bytes 4128 | tf_op jit(solution)/shard_map/ppermute | solution.py:309
  25.8 0.0 collective-permute-done.sib_ref
  25.8 0.6 stats.1
  26.3 1.9 %collective-permute-start.4 = (f32[4,512]{1,0:T(4,128)S(1)}, f32[4,512]{1,0:T(4,128)S(1)}, u32[]{:S(2)}, u32[]{:S(2)}) collective-permute-start(f32[4,512]{1,0:T(4,128)S(1)} %get-tuple-element.47.refs_4_), channel_id=1, source_target_pairs={{0,5},{2,7},{5,0},{7,2},{8,13},{10,15},{13,8},{15,10},{16,21},{18,... | collective-permute-start | bytes 24584 | tf_op jit(solution)/shard_map/ppermute | solution.py:309
  28.3 1.9 %collective-permute-start.3 = (f32[4,512]{1,0:T(4,128)S(1)}, f32[4,512]{1,0:T(4,128)S(1)}, u32[]{:S(2)}, u32[]{:S(2)}) collective-permute-start(f32[4,512]{1,0:T(4,128)S(1)} %get-tuple-element.47.refs_4_), channel_id=1, source_target_pairs={{0,9},{2,11},{4,13},{6,15},{8,17},{9,0},{10,19},{11,2},{12,21},{13... | collective-permute-start | bytes 24584 | tf_op jit(solution)/shard_map/ppermute | solution.py:309
  30.2 2.2 %copy-done.3 = bf16[4096,512]{1,0:T(8,128)(2,1)S(1)} copy-done((bf16[4096,512]{1,0:T(8,128)(2,1)S(1)}, bf16[4096,512]{1,0:T(8,128)(2,1)}, u32[]{:S(2)}) %copy-start.3) | copy-done | bytes 4194328
  32.4 4.3 %own_tile.1 = (bf16[512,4096]{1,0:T(8,128)(2,1)S(1)}, f32[256,512]{1,0:T(8,128)S(1)}, f32[256,512]{1,0:T(8,128)S(1)}) custom-call(s32[6]{0:T(128)S(1)} %stack.27.pos_ref.refs_0_, bf16[4096,512]{1,0:T(8,128)(2,1)S(1)} %copy-done.3, f32[4,512]{1,0:T(4,128)S(1)} %get-tuple-element.45.stat_ref), custom_call_target="tpu_custom_call" | custom-call | flops 2147483648 | bytes 8388608 | tf_op jit(solution)/shard_map/own_tile/pallas_call | solution.py:357
  36.7 0.0 collective-permute-done.4.refs_5_
  36.7 0.0 collective-permute-done.3.refs_6_
  36.7 1.3 %collective-permute-start.8 = (bf16[4096,256]{1,0:T(8,128)(2,1)S(1)}, bf16[4096,256]{1,0:T(8,128)(2,1)S(1)}, u32[]{:S(2)}, u32[]{:S(2)}) collective-permute-start(bf16[4096,256]{1,0:T(8,128)(2,1)S(1)} %copy-done.5), channel_id=1, source_target_pairs={{1,9},{3,11},{5,13},{7,15},{8,0},{9,17},{10,2},{11,19},{12,4},{13,... | collective-permute-start | bytes 6291464 | tf_op jit(solution)/shard_map/ppermute | solution.py:309
  38.0 1.3 %collective-permute-start.7 = (bf16[4096,256]{1,0:T(8,128)(2,1)S(1)}, bf16[4096,256]{1,0:T(8,128)(2,1)S(1)}, u32[]{:S(2)}, u32[]{:S(2)}) collective-permute-start(bf16[4096,256]{1,0:T(8,128)(2,1)S(1)} %copy-done.5), channel_id=1, source_target_pairs={{1,5},{3,7},{4,0},{6,2},{9,13},{11,15},{12,8},{14,10},{17,21},{19,... | collective-permute-start | bytes 6291464 | tf_op jit(solution)/shard_map/ppermute | solution.py:309
  39.3 0.6 collective-permute-start.9
  39.9 6.5 %pair_tiles_0.1 = (f32[6,128,128]{2,1,0:T(8,128)S(1)}, f32[6,128,128]{2,1,0:T(8,128)S(1)}, f32[9,128,128]{2,1,0:T(8,128)S(1)}, f32[9,128,128]{2,1,0:T(8,128)S(1)...) custom-call(s32[6]{0:T(128)S(1)} %stack.27.pos_ref.refs_0_, ...), custom_call_target="tpu_custom_call" | custom-call | flops 3221225472 | bytes 8388608 | tf_op jit(solution)/shard_map/pair_tiles_0/pallas_call | solution.py:385
  46.4 5.4 %collective-permute-done.9.diag_got = f32[256,512]{1,0:T(8,128)S(1)} collective-permute-done((f32[256,512]{1,0:T(8,128)S(1)}, f32[256,512]{1,0:T(8,128)S(1)}, u32[]{:S(2)}, u32[]{:S(2)}) %collective-permute-start.9) | collective-permute-done | bytes 524320 | tf_op jit(solution)/shard_map/ppermute | solution.py:309
  51.8 2.4 %collective-permute-start.10 = (f32[9,128,128]{2,1,0:T(8,128)S(1)}, f32[9,128,128]{2,1,0:T(8,128)S(1)}, u32[]{:S(2)}, u32[]{:S(2)}) collective-permute-start(f32[9,128,128]{2,1,0:T(8,128)S(1)} %get-tuple-element.61), channel_id=1, source_target_pairs={{0,2},{2,0},{5,7},{7,5},{8,10},{10,8},{13,15},{15,13},{16,18},{18,... | collective-permute-start | bytes 1769480 | tf_op jit(solution)/shard_map/ppermute | solution.py:309
  54.2 1.6 %collective-permute-start.11 = (f32[6,128,128]{2,1,0:T(8,128)S(1)}, f32[6,128,128]{2,1,0:T(8,128)S(1)}, u32[]{:S(2)}, u32[]{:S(2)}) collective-permute-start(f32[6,128,128]{2,1,0:T(8,128)S(1)} %get-tuple-element.62), channel_id=1, source_target_pairs={{0,2},{1,3},{2,0},{3,1},{4,6},{5,7},{6,4},{7,5},{8,10},{9,11},{10,... | collective-permute-start | bytes 1179656 | tf_op jit(solution)/shard_map/ppermute | solution.py:309
  55.8 8.8 %collective-permute-done.8.refs_3_ = bf16[4096,256]{1,0:T(8,128)(2,1)S(1)} collective-permute-done((bf16[4096,256]{1,0:T(8,128)(2,1)S(1)}, bf16[4096,256]{1,0:T(8,128)(2,1)S(1)}, u32[]{:S(2)}, u32[]{:S(2)}) %collective-permute-start.8) | collective-permute-done | bytes 2097184 | tf_op jit(solution)/shard_map/ppermute | solution.py:309
  64.7 1.3 %collective-permute-done.7.refs_2_ = bf16[4096,256]{1,0:T(8,128)(2,1)S(1)} collective-permute-done((bf16[4096,256]{1,0:T(8,128)(2,1)S(1)}, bf16[4096,256]{1,0:T(8,128)(2,1)S(1)}, u32[]{:S(2)}, u32[]{:S(2)}) %collective-permute-start.7) | collective-permute-done | bytes 2097184 | tf_op jit(solution)/shard_map/ppermute | solution.py:309
  66.0 7.0 %pair_tiles_1.1 = (f32[6,128,128]{2,1,0:T(8,128)S(1)}, bf16[6,128,128]{2,1,0:T(8,128)(2,1)S(1)}, f32[15,128,128]{2,1,0:T(8,128)S(1)}, bf16[15,128,128]{2,1,0:T(8,128)(2,1)S(1)}) custom-call(s32[6]{0:T(128)S(1)} %stack.27.pos_ref.refs_0_, bf16[512,4096]{1,0:T(8,128)(2,1)S(1)} %get-tuple-element.49.refs_1_, ...), custom_call_target="tpu_custom_call" | custom-call | flops 3221225472 | bytes 8388608 | tf_op jit(solution)/shard_map/pair_tiles_1/pallas_call | solution.py:385
  72.9 0.0 collective-permute-done.10.refs_4_
  72.9 2.4 %collective-permute-start.13 = (bf16[15,128,128]{2,1,0:T(8,128)(2,1)S(1)}, bf16[15,128,128]{2,1,0:T(8,128)(2,1)S(1)}, u32[]{:S(2)}, u32[]{:S(2)}) collective-permute-start(bf16[15,128,128]{2,1,0:T(8,128)(2,1)S(1)} %get-tuple-element.71), channel_id=1, source_target_pairs={{0,2},{2,0},{5,7},{7,5},{8,10},{10,8},{13,15},{15,13},{16,18},{18,... | collective-permute-start | bytes 1474568 | tf_op jit(solution)/shard_map/ppermute | solution.py:309
  75.4 1.6 %collective-permute-start.12 = (bf16[6,128,128]{2,1,0:T(8,128)(2,1)S(1)}, bf16[6,128,128]{2,1,0:T(8,128)(2,1)S(1)}, u32[]{:S(2)}, u32[]{:S(2)}) collective-permute-start(bf16[6,128,128]{2,1,0:T(8,128)(2,1)S(1)} %get-tuple-element.69), channel_id=1, source_target_pairs={{0,2},{1,3},{2,0},{3,1},{4,6},{5,7},{6,4},{7,5},{8,10},{9,11},{10,... | collective-permute-start | bytes 589832 | tf_op jit(solution)/shard_map/ppermute | solution.py:309
  77.0 0.9 strips_0.1
  77.8 2.9 %collective-permute-start.14 = (f32[128,768]{1,0:T(8,128)S(1)}, f32[128,768]{1,0:T(8,128)S(1)}, u32[]{:S(2)}, u32[]{:S(2)}) collective-permute-start(f32[128,768]{1,0:T(8,128)S(1)} %get-tuple-element.74), channel_id=1, source_target_pairs={{0,5},{2,7},{5,0},{7,2},{8,13},{10,15},{13,8},{15,10},{16,21},{18,... | collective-permute-start | bytes 1179656 | tf_op jit(solution)/shard_map/ppermute | solution.py:309
  80.7 1.9 %collective-permute-start.15 = (f32[128,768]{1,0:T(8,128)S(1)}, f32[128,768]{1,0:T(8,128)S(1)}, u32[]{:S(2)}, u32[]{:S(2)}) collective-permute-start(f32[128,768]{1,0:T(8,128)S(1)} %get-tuple-element.75), channel_id=1, source_target_pairs={{0,9},{2,11},{4,13},{6,15},{8,17},{9,0},{10,19},{11,2},{12,21},{13... | collective-permute-start | bytes 1179656 | tf_op jit(solution)/shard_map/ppermute | solution.py:309
  82.7 3.1 %collective-permute-done.12.refs_2_ = bf16[6,128,128]{2,1,0:T(8,128)(2,1)S(1)} collective-permute-done((bf16[6,128,128]{2,1,0:T(8,128)(2,1)S(1)}, bf16[6,128,128]{2,1,0:T(8,128)(2,1)S(1)}, u32[]{:S(2)}, u32[]{:S(2)}) %collective-permute-start.12) | collective-permute-done | bytes 196640 | tf_op jit(solution)/shard_map/ppermute | solution.py:309
  85.8 0.9 strips_1.1
  86.7 2.3 %collective-permute-start.16 = (bf16[128,1280]{1,0:T(8,128)(2,1)S(1)}, bf16[128,1280]{1,0:T(8,128)(2,1)S(1)}, u32[]{:S(2)}, u32[]{:S(2)}) collective-permute-start(bf16[128,1280]{1,0:T(8,128)(2,1)S(1)} %get-tuple-element.76), channel_id=1, source_target_pairs={{0,5},{2,7},{5,0},{7,2},{8,13},{10,15},{13,8},{15,10},{16,21},{18,... | collective-permute-start | bytes 983048 | tf_op jit(solution)/shard_map/ppermute | solution.py:309
  89.0 1.9 %collective-permute-start.17 = (bf16[128,1280]{1,0:T(8,128)(2,1)S(1)}, bf16[128,1280]{1,0:T(8,128)(2,1)S(1)}, u32[]{:S(2)}, u32[]{:S(2)}) collective-permute-start(bf16[128,1280]{1,0:T(8,128)(2,1)S(1)} %get-tuple-element.77), channel_id=1, source_target_pairs={{0,9},{2,11},{4,13},{6,15},{8,17},{9,0},{10,19},{11,2},{12,21},{13... | collective-permute-start | bytes 983048 | tf_op jit(solution)/shard_map/ppermute | solution.py:309
  90.9 0.0 collective-permute-done.14.y_0
  91.0 0.0 collective-permute-done.15.z_0
  91.0 4.1 %collective-permute-done.16.y_1 = bf16[128,1280]{1,0:T(8,128)(2,1)S(1)} collective-permute-done((bf16[128,1280]{1,0:T(8,128)(2,1)S(1)}, bf16[128,1280]{1,0:T(8,128)(2,1)S(1)}, u32[]{:S(2)}, u32[]{:S(2)}) %collective-permute-start.16) | collective-permute-done | bytes 327712 | tf_op jit(solution)/shard_map/ppermute | solution.py:309
  95.1 2.3 %collective-permute-done.17.z_1 = bf16[128,1280]{1,0:T(8,128)(2,1)S(1)} collective-permute-done((bf16[128,1280]{1,0:T(8,128)(2,1)S(1)}, bf16[128,1280]{1,0:T(8,128)(2,1)S(1)}, u32[]{:S(2)}, u32[]{:S(2)}) %collective-permute-start.17) | collective-permute-done | bytes 327712 | tf_op jit(solution)/shard_map/ppermute | solution.py:309
  97.4 0.8 combine.1
  98.2 0.1 collective-permute-start.18
  98.3 2.6 %collective-permute-done.18.sib = f32[4,128,512]{2,1,0:T(8,128)S(1)} collective-permute-done((f32[4,128,512]{2,1,0:T(8,128)S(1)}, f32[4,128,512]{2,1,0:T(8,128)S(1)}, u32[]{:S(2)}, u32[]{:S(2)}) %collective-permute-start.18) | collective-permute-done | bytes 1048608 | tf_op jit(solution)/shard_map/ppermute | solution.py:309
  100.9 1.7 %finish.1 = (bf16[1,3,128,512]{3,2,1,0:T(8,128)(2,1)}, bf16[1,2,128,512]{3,2,1,0:T(8,128)(2,1)}) custom-call(s32[6]{0:T(128)S(1)} %stack.27.pos_ref.refs_0_, s32[1,3]{1,0:T(1,128)S(1)} %copy-done.1, f32[4,128,512]{2,1,0:T(8,128)S(1)} %get-tuple-element.80.mine, f32[4,128,512]{2,1,0:T(8,128)S(1)} %collective-permute-done.18.sib), custom_call_target="tpu_custom_call" | custom-call | tf_op jit(solution)/shard_map/finish/pallas_call | solution.py:426
  (13 shorter events, 0.0 us)
Async XLA Ops:
  0.6 6.8 %copy-start = (bf16[4096,512]{1,0:T(8,128)(2,1)S(1)}, bf16[4096,512]{1,0:T(8,128)(2,1)}, u32[]{:S(2)}) copy-start(bf16[4096,512]{1,0:T(8,128)(2,1)} %refs_0_) | copy-start | bytes 12582916
  4.7 21.1 %copy-start.1 = (s32[1,3]{1,0:T(1,128)S(1)}, s32[1,3]{1,0:T(1,128)}, u32[]{:S(2)}) copy-start(s32[1,3]{1,0:T(1,128)} %offsets_ref.3) | copy-start | bytes 40
  4.7 35.2 %collective-permute-start.6 = (bf16[4096,256]{1,0:T(8,128)(2,1)}, bf16[4096,256]{1,0:T(8,128)(2,1)}, u32[]{:S(2)}, u32[]{:S(2)}) collective-permute-start(bf16[4096,256]{1,0:T(8,128)(2,1)} %first_chunk.1), channel_id=1, source_target_pairs={{1,9},{3,11},{5,13},{7,15},{8,0},{9,17},{10,2},{11,19},{12,4},{13,... | collective-permute-start | bytes 6291464 | tf_op jit(solution)/shard_map/ppermute | solution.py:309
  6.1 33.8 %collective-permute-start.5 = (bf16[4096,256]{1,0:T(8,128)(2,1)}, bf16[4096,256]{1,0:T(8,128)(2,1)}, u32[]{:S(2)}, u32[]{:S(2)}) collective-permute-start(bf16[4096,256]{1,0:T(8,128)(2,1)} %first_chunk.1), channel_id=1, source_target_pairs={{1,5},{3,7},{4,0},{6,2},{9,13},{11,15},{12,8},{14,10},{17,21},{19,... | collective-permute-start | bytes 6291464 | tf_op jit(solution)/shard_map/ppermute | solution.py:309
  10.0 2.0 %copy-start.2 = (bf16[4096,512]{1,0:T(8,128)(2,1)}, bf16[4096,512]{1,0:T(8,128)(2,1)S(1)}, u32[]{:S(2)}) copy-start(bf16[4096,512]{1,0:T(8,128)(2,1)S(1)} %get-tuple-element.43.x_ref) | copy-start | bytes 12582916
  11.9 1.4 %copy-start.4 = (bf16[4096,256]{1,0:T(8,128)(2,1)}, bf16[4096,256]{1,0:T(8,128)(2,1)S(1)}, u32[]{:S(2)}) copy-start(bf16[4096,256]{1,0:T(8,128)(2,1)S(1)} %get-tuple-element.53) | copy-start | bytes 6291460
  13.3 10.2 %collective-permute-start.2 = (f32[2,512]{1,0:T(2,128)S(1)}, f32[2,512]{1,0:T(2,128)S(1)}, u32[]{:S(2)}, u32[]{:S(2)}) collective-permute-start(f32[2,512]{1,0:T(2,128)S(1)} %get-tuple-element.44.own_ref), channel_id=1, source_target_pairs={{0,3},{1,2},{2,1},{3,0},{4,7},{5,6},{6,5},{7,4},{8,11},{9,10},{10,... | collective-permute-start | bytes 12296 | tf_op jit(solution)/shard_map/ppermute | solution.py:309
  22.1 3.6 %collective-permute-start.1 = (f32[2,512]{1,0:T(2,128)S(1)}, f32[2,512]{1,0:T(2,128)S(1)}, u32[]{:S(2)}, u32[]{:S(2)}) collective-permute-start(f32[2,512]{1,0:T(2,128)S(1)} %get-tuple-element.44.own_ref), channel_id=1, source_target_pairs={{0,2},{1,3},{2,0},{3,1},{4,6},{5,7},{6,4},{7,5},{8,10},{9,11},{10,... | collective-permute-start | bytes 12296 | tf_op jit(solution)/shard_map/ppermute | solution.py:309
  22.7 3.1 %collective-permute-start = (f32[2,512]{1,0:T(2,128)S(1)}, f32[2,512]{1,0:T(2,128)S(1)}, u32[]{:S(2)}, u32[]{:S(2)}) collective-permute-start(f32[2,512]{1,0:T(2,128)S(1)} %get-tuple-element.44.own_ref), channel_id=1, source_target_pairs={{0,1},{1,0},{2,3},{3,2},{4,5},{5,4},{6,7},{7,6},{8,9},{9,8},{10,11... | collective-permute-start | bytes 12296 | tf_op jit(solution)/shard_map/ppermute | solution.py:309
  26.3 10.4 %collective-permute-start.4 = (f32[4,512]{1,0:T(4,128)S(1)}, f32[4,512]{1,0:T(4,128)S(1)}, u32[]{:S(2)}, u32[]{:S(2)}) collective-permute-start(f32[4,512]{1,0:T(4,128)S(1)} %get-tuple-element.47.refs_4_), channel_id=1, source_target_pairs={{0,5},{2,7},{5,0},{7,2},{8,13},{10,15},{13,8},{15,10},{16,21},{18,... | collective-permute-start | bytes 24584 | tf_op jit(solution)/shard_map/ppermute | solution.py:309
  28.3 8.5 %collective-permute-start.3 = (f32[4,512]{1,0:T(4,128)S(1)}, f32[4,512]{1,0:T(4,128)S(1)}, u32[]{:S(2)}, u32[]{:S(2)}) collective-permute-start(f32[4,512]{1,0:T(4,128)S(1)} %get-tuple-element.47.refs_4_), channel_id=1, source_target_pairs={{0,9},{2,11},{4,13},{6,15},{8,17},{9,0},{10,19},{11,2},{12,21},{13... | collective-permute-start | bytes 24584 | tf_op jit(solution)/shard_map/ppermute | solution.py:309
  30.2 2.2 %copy-start.3 = (bf16[4096,512]{1,0:T(8,128)(2,1)S(1)}, bf16[4096,512]{1,0:T(8,128)(2,1)}, u32[]{:S(2)}) copy-start(bf16[4096,512]{1,0:T(8,128)(2,1)} %copy-done.2) | copy-start | bytes 12582916
  32.4 4.3 %copy-start.5 = (bf16[4096,256]{1,0:T(8,128)(2,1)S(1)}, bf16[4096,256]{1,0:T(8,128)(2,1)}, u32[]{:S(2)}) copy-start(bf16[4096,256]{1,0:T(8,128)(2,1)} %copy-done.4) | copy-start | bytes 6291460
  36.7 27.9 %collective-permute-start.8 = (bf16[4096,256]{1,0:T(8,128)(2,1)S(1)}, bf16[4096,256]{1,0:T(8,128)(2,1)S(1)}, u32[]{:S(2)}, u32[]{:S(2)}) collective-permute-start(bf16[4096,256]{1,0:T(8,128)(2,1)S(1)} %copy-done.5), channel_id=1, source_target_pairs={{1,9},{3,11},{5,13},{7,15},{8,0},{9,17},{10,2},{11,19},{12,4},{13,... | collective-permute-start | bytes 6291464 | tf_op jit(solution)/shard_map/ppermute | solution.py:309
  38.0 27.9 %collective-permute-start.7 = (bf16[4096,256]{1,0:T(8,128)(2,1)S(1)}, bf16[4096,256]{1,0:T(8,128)(2,1)S(1)}, u32[]{:S(2)}, u32[]{:S(2)}) collective-permute-start(bf16[4096,256]{1,0:T(8,128)(2,1)S(1)} %copy-done.5), channel_id=1, source_target_pairs={{1,5},{3,7},{4,0},{6,2},{9,13},{11,15},{12,8},{14,10},{17,21},{19,... | collective-permute-start | bytes 6291464 | tf_op jit(solution)/shard_map/ppermute | solution.py:309
  39.3 12.5 %collective-permute-start.9 = (f32[256,512]{1,0:T(8,128)S(1)}, f32[256,512]{1,0:T(8,128)S(1)}, u32[]{:S(2)}, u32[]{:S(2)}) collective-permute-start(f32[256,512]{1,0:T(8,128)S(1)} %get-tuple-element.60), channel_id=1, source_target_pairs={{0,2},{1,3},{2,0},{3,1},{4,6},{5,7},{6,4},{7,5},{8,10},{9,11},{10,... | collective-permute-start | bytes 1572872 | tf_op jit(solution)/shard_map/ppermute | solution.py:309
  51.8 21.1 %collective-permute-start.10 = (f32[9,128,128]{2,1,0:T(8,128)S(1)}, f32[9,128,128]{2,1,0:T(8,128)S(1)}, u32[]{:S(2)}, u32[]{:S(2)}) collective-permute-start(f32[9,128,128]{2,1,0:T(8,128)S(1)} %get-tuple-element.61), channel_id=1, source_target_pairs={{0,2},{2,0},{5,7},{7,5},{8,10},{10,8},{13,15},{15,13},{16,18},{18,... | collective-permute-start | bytes 1769480 | tf_op jit(solution)/shard_map/ppermute | solution.py:309
  54.2 18.7 %collective-permute-start.11 = (f32[6,128,128]{2,1,0:T(8,128)S(1)}, f32[6,128,128]{2,1,0:T(8,128)S(1)}, u32[]{:S(2)}, u32[]{:S(2)}) collective-permute-start(f32[6,128,128]{2,1,0:T(8,128)S(1)} %get-tuple-element.62), channel_id=1, source_target_pairs={{0,2},{1,3},{2,0},{3,1},{4,6},{5,7},{6,4},{7,5},{8,10},{9,11},{10,... | collective-permute-start | bytes 1179656 | tf_op jit(solution)/shard_map/ppermute | solution.py:309
  72.9 12.8 %collective-permute-start.13 = (bf16[15,128,128]{2,1,0:T(8,128)(2,1)S(1)}, bf16[15,128,128]{2,1,0:T(8,128)(2,1)S(1)}, u32[]{:S(2)}, u32[]{:S(2)}) collective-permute-start(bf16[15,128,128]{2,1,0:T(8,128)(2,1)S(1)} %get-tuple-element.71), channel_id=1, source_target_pairs={{0,2},{2,0},{5,7},{7,5},{8,10},{10,8},{13,15},{15,13},{16,18},{18,... | collective-permute-start | bytes 1474568 | tf_op jit(solution)/shard_map/ppermute | solution.py:309
  75.4 10.4 %collective-permute-start.12 = (bf16[6,128,128]{2,1,0:T(8,128)(2,1)S(1)}, bf16[6,128,128]{2,1,0:T(8,128)(2,1)S(1)}, u32[]{:S(2)}, u32[]{:S(2)}) collective-permute-start(bf16[6,128,128]{2,1,0:T(8,128)(2,1)S(1)} %get-tuple-element.69), channel_id=1, source_target_pairs={{0,2},{1,3},{2,0},{3,1},{4,6},{5,7},{6,4},{7,5},{8,10},{9,11},{10,... | collective-permute-start | bytes 589832 | tf_op jit(solution)/shard_map/ppermute | solution.py:309
  77.8 13.1 %collective-permute-start.14 = (f32[128,768]{1,0:T(8,128)S(1)}, f32[128,768]{1,0:T(8,128)S(1)}, u32[]{:S(2)}, u32[]{:S(2)}) collective-permute-start(f32[128,768]{1,0:T(8,128)S(1)} %get-tuple-element.74), channel_id=1, source_target_pairs={{0,5},{2,7},{5,0},{7,2},{8,13},{10,15},{13,8},{15,10},{16,21},{18,... | collective-permute-start | bytes 1179656 | tf_op jit(solution)/shard_map/ppermute | solution.py:309
  80.7 10.2 %collective-permute-start.15 = (f32[128,768]{1,0:T(8,128)S(1)}, f32[128,768]{1,0:T(8,128)S(1)}, u32[]{:S(2)}, u32[]{:S(2)}) collective-permute-start(f32[128,768]{1,0:T(8,128)S(1)} %get-tuple-element.75), channel_id=1, source_target_pairs={{0,9},{2,11},{4,13},{6,15},{8,17},{9,0},{10,19},{11,2},{12,21},{13... | collective-permute-start | bytes 1179656 | tf_op jit(solution)/shard_map/ppermute | solution.py:309
  86.7 8.4 %collective-permute-start.16 = (bf16[128,1280]{1,0:T(8,128)(2,1)S(1)}, bf16[128,1280]{1,0:T(8,128)(2,1)S(1)}, u32[]{:S(2)}, u32[]{:S(2)}) collective-permute-start(bf16[128,1280]{1,0:T(8,128)(2,1)S(1)} %get-tuple-element.76), channel_id=1, source_target_pairs={{0,5},{2,7},{5,0},{7,2},{8,13},{10,15},{13,8},{15,10},{16,21},{18,... | collective-permute-start | bytes 983048 | tf_op jit(solution)/shard_map/ppermute | solution.py:309
  89.0 8.4 %collective-permute-start.17 = (bf16[128,1280]{1,0:T(8,128)(2,1)S(1)}, bf16[128,1280]{1,0:T(8,128)(2,1)S(1)}, u32[]{:S(2)}, u32[]{:S(2)}) collective-permute-start(bf16[128,1280]{1,0:T(8,128)(2,1)S(1)} %get-tuple-element.77), channel_id=1, source_target_pairs={{0,9},{2,11},{4,13},{6,15},{8,17},{9,0},{10,19},{11,2},{12,21},{13... | collective-permute-start | bytes 983048 | tf_op jit(solution)/shard_map/ppermute | solution.py:309
  98.2 2.7 %collective-permute-start.18 = (f32[4,128,512]{2,1,0:T(8,128)S(1)}, f32[4,128,512]{2,1,0:T(8,128)S(1)}, u32[]{:S(2)}, u32[]{:S(2)}) collective-permute-start(f32[4,128,512]{2,1,0:T(8,128)S(1)} %get-tuple-element.81), channel_id=1, source_target_pairs={{0,1},{1,0},{2,3},{3,2},{4,5},{5,4},{6,7},{7,6},{8,9},{9,8},{10,11... | collective-permute-start | bytes 3145736 | tf_op jit(solution)/shard_map/ppermute | solution.py:309
